TPU v7x, 768 devices: a whole 4x8x12 slice. The times are simulated.
768 devices in a mesh: dp: 96 (over y_hi, z, core), fsdp: 8 (over y_lo, x).
Axes of the slice: x: 4, y: 8 (y_hi: 4, y_lo: 2; y = y_hi * 2 + y_lo), z: 12, core: 2. Of those that a mesh axis runs over, the one named last changes fastest.
Arguments:
- features: bfloat16 [135168, 832], P(('dp', 'fsdp')), may hold values from -6 to 6
- head_weight: bfloat16 [832, 1024], P('fsdp'), may hold values from -0.21875 to 0.21875
- text_embed: bfloat16 [135168, 1024], P(('dp', 'fsdp')), may hold values from -1.5 to 1.5
Outputs:
- loss: float32 [], replicated
- feat_grad: bfloat16 [135168, 832], P(('dp', 'fsdp'))
- text_grad: bfloat16 [135168, 1024], P(('dp', 'fsdp'))
- head_grad: float32 [832, 1024], P('fsdp')
All inputs are finite; a program needn't handle non-finite values.
Results may differ from a plain program's by a relative error of at most 0.011.
Values may be sent and summed in bfloat16 or wider, within the bound.
No kernel may reach another device: no remote copies, remote signals or barrier semaphores. Data moves between devices by JAX's collectives and lax.ppermute only.
A program may use at most 32 MiB of HBM per device.

v0:
```python
import jax
import jax.numpy as jnp
from jax import lax
from jax.sharding import PartitionSpec as P


def unit_rows(vectors):
    inverse = lax.rsqrt(jnp.sum(vectors * vectors, axis=-1, keepdims=True) + 1e-06)
    return (vectors * inverse, inverse)


def row_lse(values):
    peak = jnp.max(values, axis=1)
    return peak + jnp.log(jnp.sum(jnp.exp(values - peak[:, None]), axis=1))


def left_product(left, right):
    return lax.dot_general(
        left, right, (((0,), (0,)), ((), ())), preferred_element_type=jnp.float32
    )


def right_product(left, right):
    return lax.dot_general(
        left, right, (((1,), (1,)), ((), ())), preferred_element_type=jnp.float32
    )


def body(features, head_weight, text_embed):
    weight = lax.all_gather(head_weight, "fsdp", axis=0, tiled=True)
    z_rows = jnp.dot(features, weight, preferred_element_type=jnp.float32)
    u_rows, inv_u = unit_rows(z_rows)
    image_unit = u_rows.astype(jnp.bfloat16)
    v_rows, inv_v = unit_rows(text_embed.astype(jnp.float32))
    text_unit = v_rows.astype(jnp.bfloat16)
    rows = features.shape[0]
    first = lax.axis_index("fsdp") * rows
    image_all, text_all = (
        lax.all_gather(image_unit, "fsdp", axis=0, tiled=True),
        lax.all_gather(text_unit, "fsdp", axis=0, tiled=True),
    )
    group = text_all.shape[0]
    onehot = (
        lax.broadcasted_iota(jnp.int32, (rows, group), 1)
        == first + lax.broadcasted_iota(jnp.int32, (rows, group), 0)
    ).astype(jnp.float32)
    row_scores = 100.0 * right_product(image_unit, text_all)
    col_scores = 100.0 * right_product(text_unit, image_all)
    lse_row = row_lse(row_scores)
    lse_col = row_lse(col_scores)
    lse_row_all, lse_col_all = (
        lax.all_gather(lse_row, "fsdp", axis=0, tiled=True),
        lax.all_gather(lse_col, "fsdp", axis=0, tiled=True),
    )
    row_coupling = (
        jnp.exp(row_scores - lse_row[:, None])
        + jnp.exp(row_scores - lse_col_all[None, :])
        - 2.0 * onehot
    ).astype(jnp.bfloat16)
    col_coupling = (
        jnp.exp(col_scores - lse_row_all[None, :])
        + jnp.exp(col_scores - lse_col[:, None])
        - 2.0 * onehot
    ).astype(jnp.bfloat16)
    du_rows = 100.0 * jnp.dot(row_coupling, text_all, preferred_element_type=jnp.float32)
    dv_rows = 100.0 * jnp.dot(col_coupling, image_all, preferred_element_type=jnp.float32)
    diagonal = jnp.sum(row_scores * onehot, axis=1)
    local_loss = jnp.sum(lse_row - diagonal) + jnp.sum(lse_col - diagonal)
    total_pairs = group * lax.axis_size("dp")
    loss = lax.psum(local_loss, ("dp", "fsdp")) / (2.0 * total_pairs)
    dz_local = (
        (du_rows - u_rows * jnp.sum(u_rows * du_rows, axis=-1, keepdims=True)) * inv_u
    ).astype(jnp.bfloat16)
    text_grad = (
        (dv_rows - v_rows * jnp.sum(v_rows * dv_rows, axis=-1, keepdims=True)) * inv_v
    ).astype(jnp.bfloat16)
    feat_grad = right_product(dz_local, weight).astype(jnp.bfloat16)
    head_part = lax.psum_scatter(
        left_product(features, dz_local), "fsdp", scatter_dimension=0, tiled=True
    )
    head_grad = lax.psum(head_part, "dp")
    return (loss, feat_grad, text_grad, head_grad)


def solution(mesh):
    in_specs = (P(("dp", "fsdp"), None), P("fsdp", None), P(("dp", "fsdp"), None))
    out_specs = (P(), P(("dp", "fsdp"), None), P(("dp", "fsdp"), None), P("fsdp", None))
    return jax.shard_map(body, mesh=mesh, in_specs=in_specs, out_specs=out_specs, check_vma=False)
```

profile of v0, /device:TPU:1, one launch (start us, length us, event | category | flops | bytes accessed | tf_op | source)
XLA Modules:
  0.0 1113.5 jit_solution(2213767052358511555)
XLA Ops:
  7.2 0.0 copy-start
  7.2 0.0 all-gather.4.cloned.1.call-start
  7.2 0.7 all-gather.4.cloned.1.call-update
  7.9 0.0 all-gather.6.cloned.1.call-start
  8.0 1.1 fusion.9
  9.1 1.9 fusion.4
  11.0 0.0 all-gather.6.cloned.1.call-update
  11.0 0.0 all-gather.8.cloned.1.call-start
  11.0 50.1 %all-gather.4.cloned.1.call-done = bf16[832,1024]{1,0:T(8,128)(2,1)} async-done(((bf16[104,1024]{1,0:T(8,128)(2,1)}), bf16[832,1024]{1,0:T(8,128)(2,1)}) %all-gather.4.cloned.1.call-update) | async-done | bytes 1703952 | tf_op jit(solution)/shard_map/all_gather | solution.py:30
  61.2 0.0 copy-done
  61.2 2.1 multiply_reduce_fusion.1
  63.3 0.9 multiply_convert_fusion.1
  64.1 0.0 copy-start.2
  64.1 0.0 all-gather.8.cloned.1.call-update
  64.2 0.0 reduce-scatter.2.cloned.1.call-start
  64.2 1.3 dynamic-slice
  66.2 51.1 %all-gather.6.cloned.1.call-done = bf16[1408,1024]{1,0:T(8,128)(2,1)} async-done(((bf16[176,1024]{1,0:T(8,128)(2,1)}), bf16[1408,1024]{1,0:T(8,128)(2,1)}) %all-gather.6.cloned.1.call-update) | async-done | bytes 2883600 | tf_op jit(solution)/shard_map/all_gather | solution.py:40
  117.3 4.1 fusion.29
  121.4 1.7 select_reduce_fusion
  123.1 0.1 fusion.26
  123.2 47.7 %all-gather.8.cloned.1.call-done = bf16[1408,1024]{1,0:T(8,128)(2,1)} async-done(((bf16[176,1024]{1,0:T(8,128)(2,1)}), bf16[1408,1024]{1,0:T(8,128)(2,1)}) %all-gather.8.cloned.1.call-update) | async-done | bytes 2883600 | tf_op jit(solution)/shard_map/all_gather | solution.py:39
  170.9 0.0 copy-done.2
  170.9 3.0 fusion.28
  173.9 0.3 exponential_reduce_fusion
  174.2 0.1 fusion.27
  174.3 26.1 %all-reduce.2 = (f32[1408]{0:T(1024)S(1)}, f32[1408]{0:T(1024)S(1)}) all-reduce(f32[1408]{0:T(1024)S(1)} %get-tuple-element.12, f32[1408]{0:T(1024)S(1)} %get-tuple-element.10), channel_id=1, replica_groups=mesh['dp'=96,'fsdp'=8] {'fsdp'}, use_global_device_ids=true, to_apply=%add | all-reduce | flops 2816 | bytes 22528
  200.4 3.2 multiply_reduce_fusion
  203.6 0.2 multiply_convert_fusion
  203.8 2.4 convolution_bitcast_fusion
  206.2 0.0 reduce-scatter.2.cloned.1.call-update
  206.2 0.0 all-reduce.5.cloned.1.call-start
  206.3 0.6 subtract_reduce_fusion
  208.2 129.5 %psum.14 = f32[]{:T(128)} all-reduce(f32[]{:T(128)S(6)} %add.58), channel_id=1, replica_groups=mesh['dp'=96,'fsdp'=8] {'dp','fsdp'}, use_global_device_ids=true, to_apply=%region_9.0 | all-reduce | flops 1 | bytes 8 | tf_op jit(solution)/shard_map/psum | solution.py:70
  338.3 0.0 copy-start.1
  338.3 3.9 fusion.5
  342.2 0.0 reduce-scatter.2.cloned.1.call-done
  342.2 0.0 all-reduce.5.cloned.1.call-update
  342.2 2.2 fusion.8
  344.4 0.0 copy-done.1
  344.4 1.5 convolution_convert_fusion
  345.8 758.2 %all-reduce.5.cloned.1.call-done = f32[104,1024]{1,0:T(8,128)} async-done(((f32[104,1024]{1,0:T(8,128)}), f32[104,1024]{1,0:T(8,128)}) %all-reduce.5.cloned.1.call-update) | async-done | bytes 426000 | tf_op jit(solution)/shard_map/psum | solution.py:81
  1104.0 1.8 copy.10
  (5 shorter events, 0.0 us)
Async XLA Ops:
  7.2 54.0 %copy-start = (bf16[176,832]{1,0:T(8,128)(2,1)S(1)}, bf16[176,832]{1,0:T(8,128)(2,1)}, u32[]{:S(2)}) copy-start(bf16[176,832]{1,0:T(8,128)(2,1)} %param.3) | copy-start | bytes 878596
  7.2 54.0 %all-gather.4.cloned.1.call-start = ((), (), s32[]{:S(2)}) async-start(), calls=%async_computation.1 | async-start | bytes 1916928 | tf_op jit(solution)/shard_map/all_gather | solution.py:30
  7.9 109.4 %all-gather.6.cloned.1.call-start = ((), (), s32[]{:S(2)}) async-start(), calls=%async_computation.2 | async-start | bytes 3244032 | tf_op jit(solution)/shard_map/all_gather | solution.py:40
  11.0 159.9 %all-gather.8.cloned.1.call-start = ((), (), s32[]{:S(2)}) async-start(), calls=%async_computation.3 | async-start | bytes 3244032 | tf_op jit(solution)/shard_map/all_gather | solution.py:39
  64.1 106.8 %copy-start.2 = (bf16[176,1024]{1,0:T(8,128)(2,1)S(1)}, bf16[176,1024]{1,0:T(8,128)(2,1)}, u32[]{:S(2)}) copy-start(bf16[176,1024]{1,0:T(8,128)(2,1)} %fusion.4) | copy-start | bytes 1081348
  64.2 278.0 %reduce-scatter.2.cloned.1.call-start = ((), (), s32[]{:S(2)}) async-start(), calls=%async_computation.4 | async-start | bytes 3833856 | tf_op jit(solution)/shard_map/reduce_scatter | solution.py:78
  206.2 897.8 %all-reduce.5.cloned.1.call-start = ((), (), s32[]{:S(2)}) async-start(), calls=%async_computation.5 | async-start | bytes 851968 | tf_op jit(solution)/shard_map/psum | solution.py:81
  338.3 6.1 copy-start.1
Sparse Core Ops, SparseCore 0:
  10.4 50.7 all-gather.3
  64.1 53.1 all-gather.5
  120.2 50.6 all-gather.7
  206.3 59.9 reduce-scatter.1
  342.3 761.6 all-reduce.4
where the time goes:
time: 1120 us; the launch traced here: 1110 us
  waiting for transfers between devices  908 us (81%)
  blocking collectives  156 us (14%)
  matrix products  20.2 us (2%)
  between operations  17.6 us (2%)
    psum x1, waiting for transfers between devices, body(): head_grad = lax.psum(head_part, 'dp')  758 us
    psum x1, blocking collectives, body(): loss = lax.psum(local_loss, ('dp', 'fsdp')) / (2.0 * total_pairs)  129 us
    all_gather x1, waiting for transfers between devices, body(): lax.all_gather(text_unit, 'fsdp', axis=0, tiled=True)  51.1 us
    all_gather x1, waiting for transfers between devices, body(): weight = lax.all_gather(head_weight, 'fsdp', axis=0, tiled=True)  50.1 us
    all_gather x1, waiting for transfers between devices, body(): lax.all_gather(image_unit, 'fsdp', axis=0, tiled=True)  47.7 us
    unnamed x1, blocking collectives  26.1 us
  transfers between devices with their start and end apart: 5, of which 4 were waited for; matrix products, arithmetic and copies ran while one was open for 2% of the time, Pallas kernels for 0%

commit v1 on v0

v1 whole, which is shorter than its diff:
```python
import jax
import jax.numpy as jnp
from jax import lax
from jax.sharding import Mesh, PartitionSpec as P

BF = jnp.bfloat16
F32 = jnp.float32


def left_product(left, right):
    return lax.dot_general(
        left, right, (((0,), (0,)), ((), ())), preferred_element_type=F32
    )


def right_product(left, right):
    return lax.dot_general(
        left, right, (((1,), (1,)), ((), ())), preferred_element_type=F32
    )


def unit_rows(vectors):
    inverse = lax.rsqrt(jnp.sum(vectors * vectors, axis=-1, keepdims=True) + 1e-06)
    return (vectors * inverse, inverse)


def ring(size, step):
    return [(i, (i + step) % size) for i in range(size)]


def gather_group(block, n_y, n_x):
    flip, up, down = ring(n_y, 1), ring(n_x, 1), ring(n_x, -1)
    rows = block.shape[0]
    half = rows // 2 // 16 * 16
    got = {(0, 0): block}
    got[1, 0] = lax.ppermute(block, "yl", flip)
    got[0, 3] = lax.ppermute(block, "x", up)
    got[0, 1] = lax.ppermute(block, "x", down)
    got[1, 3] = lax.ppermute(got[0, 3], "yl", flip)
    got[1, 1] = lax.ppermute(got[1, 0], "x", down)
    got[0, 2] = lax.ppermute(got[0, 3], "x", up)
    low = lax.ppermute(got[1, 3][:half], "x", up)
    high = lax.ppermute(got[1, 1][half:], "x", down)
    got[1, 2] = jnp.concatenate([low, high], axis=0)
    return got


def compute(weight, features, texts, own, columns):
    group = features.shape[0]
    rows = group // 8
    z_rows = jnp.dot(features, weight, preferred_element_type=F32)
    u_rows, inv_u = unit_rows(z_rows)
    image_unit = u_rows.astype(BF)
    v_rows, _ = unit_rows(texts.astype(F32))
    text_unit = v_rows.astype(BF)
    scores = 100.0 * right_product(image_unit, text_unit)
    row_peak = jnp.max(scores, axis=1)
    col_peak = jnp.max(scores, axis=0)
    lse_row = row_peak + jnp.log(jnp.sum(jnp.exp(scores - row_peak[:, None]), axis=1))
    lse_col = col_peak + jnp.log(jnp.sum(jnp.exp(scores - col_peak[None, :]), axis=0))
    eye = (
        lax.broadcasted_iota(jnp.int32, (group, group), 0)
        == lax.broadcasted_iota(jnp.int32, (group, group), 1)
    ).astype(F32)
    diagonal = jnp.sum(scores * eye, axis=1)
    loss = jnp.sum(lse_row - diagonal) + jnp.sum(lse_col - diagonal)
    coupling = (
        jnp.exp(scores - lse_row[:, None])
        + jnp.exp(scores - lse_col[None, :])
        - 2.0 * eye
    ).astype(BF)
    du = 100.0 * jnp.dot(coupling, text_unit, preferred_element_type=F32)
    dz = ((du - u_rows * jnp.sum(u_rows * du, axis=-1, keepdims=True)) * inv_u).astype(BF)
    first = own * rows
    own_coupling = lax.dynamic_slice(coupling, (0, first), (group, rows))
    dv = 100.0 * left_product(own_coupling, image_unit)
    own_text = lax.dynamic_slice(texts, (first, 0), (rows, texts.shape[1]))
    v_own, inv_v = unit_rows(own_text.astype(F32))
    text_grad = ((dv - v_own * jnp.sum(v_own * dv, axis=-1, keepdims=True)) * inv_v).astype(BF)
    dz_own = lax.dynamic_slice(dz, (first, 0), (rows, dz.shape[1]))
    feat_grad = right_product(dz_own, weight).astype(BF)
    own_features = lax.dynamic_slice(features, (0, own * columns), (group, columns))
    head = left_product(own_features, dz)
    return loss, feat_grad, text_grad, head


def pieces(value):
    one = value.astype(BF)
    two = (value - one.astype(F32)).astype(BF)
    three = (value - one.astype(F32) - two.astype(F32)).astype(BF)
    return one, two, three


def loss_rows(loss, width):
    lane = lax.broadcasted_iota(jnp.int32, (16, width), 1)
    row = lax.broadcasted_iota(jnp.int32, (16, width), 0)
    out = jnp.zeros((16, width), BF)
    for k, piece in enumerate(pieces(loss)):
        out = jnp.where((lane == k) & (row == 0), piece, out)
    return out


def sum_over_groups(head, loss, n_h, n_z):
    rows, width = head.shape
    core = lax.axis_index("core")
    padded = -(-rows // 16) * 16
    half = width // 2
    top = jnp.pad(head, ((0, padded - rows), (0, 0))).astype(BF)
    first, second = top[:, :half], top[:, half:]
    tail = loss_rows(loss, half)
    mine = jnp.where(core == 0, first, second)
    other = jnp.where(core == 0, second, first)
    other = jnp.concatenate([other, tail], axis=0)
    came = lax.ppermute(other, "core", [(0, 1), (1, 0)])
    both = (mine.astype(F32) + came[:padded].astype(F32)).astype(BF)
    chip_loss = loss + jnp.sum(came[padded].astype(F32)[:3])
    both = jnp.concatenate([both, loss_rows(chip_loss, half)], axis=0)
    lanes = half // 128
    groups = both.shape[0] // 16
    tiles = both.reshape(groups, 16, lanes, 128).transpose(0, 2, 1, 3).reshape(-1, 16, 128)
    peers = n_h * n_z
    count = tiles.shape[0]
    each = -(-count // peers)
    tiles = jnp.pad(tiles, ((0, each * peers - count), (0, 0), (0, 0)))
    tiles = lax.all_to_all(tiles, ("yh", "z"), 0, 0, tiled=True)
    total = jnp.sum(tiles.reshape(peers, each, 16, 128).astype(F32), axis=0)
    loss_tile = count - lanes
    place = (lax.axis_index("yh") * n_z + lax.axis_index("z")) * each
    here = (place + lax.broadcasted_iota(jnp.int32, (each, 16, 128), 0)) == loss_tile
    row = lax.broadcasted_iota(jnp.int32, (each, 16, 128), 1)
    one, two, three = pieces(total[:, :1])
    send = total.astype(BF)
    send = jnp.where(here & (row == 1), two, send)
    send = jnp.where(here & (row == 2), three, send)
    send = jnp.broadcast_to(send[None], (peers, each, 16, 128)).reshape(-1, 16, 128)
    tiles = lax.all_to_all(send, ("yh", "z"), 0, 0, tiled=True)
    loss = jnp.sum(tiles[loss_tile][:3, :3].astype(F32))
    tiles = tiles[: (padded // 16) * lanes].reshape(padded // 16, lanes, 16, 128)
    part = tiles.transpose(0, 2, 1, 3).reshape(padded, half)
    whole = lax.all_gather(part, "core", axis=1, tiled=True)
    return whole[:rows].astype(F32), loss


def solution(mesh):
    n_dp, n_fs = mesh.devices.shape
    n_x, n_y = 4, 2
    n_h = 4 if n_dp % 8 == 0 else 1
    n_z = n_dp // (2 * n_h)
    fine = Mesh(
        mesh.devices.reshape(n_h, n_z, 2, n_y, n_x), ("yh", "z", "core", "yl", "x")
    )
    every = ("yh", "z", "core", "yl", "x")
    part = ("yl", "x")

    def body(features, head_weight, text_embed):
        rows, depth = features.shape
        width = text_embed.shape[1]
        weight = lax.all_gather(head_weight, part, axis=0, tiled=True)
        packed = jnp.concatenate([text_embed, features], axis=1)
        packed = jnp.pad(packed, ((0, 0), (0, -packed.shape[1] % 128)))
        got = gather_group(packed, n_y, n_x)
        y, x = lax.axis_index("yl"), lax.axis_index("x")
        texts = jnp.zeros((n_fs * rows, width), BF)
        all_features = jnp.zeros((n_fs * rows, depth), BF)
        for (dy, dx), block in got.items():
            place = (((y + dy) % n_y) * n_x + (x + dx) % n_x) * rows
            texts = lax.dynamic_update_slice(texts, block[:, :width], (place, 0))
            all_features = lax.dynamic_update_slice(
                all_features, block[:, width : width + depth], (place, 0)
            )
        own = y * n_x + x
        loss, feat_grad, text_grad, head = compute(
            weight, all_features, texts, own, head_weight.shape[0]
        )
        head_grad, loss = sum_over_groups(head, loss, n_h, n_z)
        loss = loss / (2.0 * n_fs * rows * n_dp)
        return (loss, feat_grad, text_grad, head_grad)

    in_specs = (P(every, None), P(part, None), P(every, None))
    out_specs = (P(), P(every, None), P(every, None), P(part, None))
    return jax.shard_map(
        body, mesh=fine, in_specs=in_specs, out_specs=out_specs, check_vma=False
    )
```

time: 1120 us -> 199 us (0.18)
  waiting for transfers between devices: 908 us -> 41.7 us
  blocking collectives: 156 us -> 5.45 us
  starting transfers between devices: 0.2 us -> 68.7 us
  local copies, waits for them, and re-layouts: 3.12 us -> 17.3 us
  other arithmetic: 9.02 us -> 20.5 us
    psum x1 -> x0, waiting for transfers between devices: 758 us -> none  [body(): head_grad = lax.psum(head_part, 'dp')]
    all_gather x3 -> x1, waiting for transfers between devices: 149 us -> 0.01 us  [body(): weight = lax.all_gather(head_weight, part, axis=0, tiled=True)]
    psum x1 -> x0, blocking collectives: 129 us -> none  [body(): loss = lax.psum(local_loss, ('dp', 'fsdp')) / (2.0 * total_pairs)]
    ppermute x0 -> x9, starting transfers between devices: none -> 41.3 us  [the longest x1 9.76 us: gather_group(): got[1, 3] = lax.ppermute(got[0, 3], 'yl', flip)]
    all_to_all x0 -> x2, starting transfers between devices: none -> 27.3 us  [the longest x1 21.7 us: sum_over_groups(): tiles = lax.all_to_all(tiles, ('yh', 'z'), 0, 0, tiled=True)]
    unnamed x1 -> x0, blocking collectives: 26.1 us -> none
    all_to_all x0 -> x2, waiting for transfers between devices: none -> 24.2 us  [the longest x1 16.2 us: sum_over_groups(): tiles = lax.all_to_all(tiles, ('yh', 'z'), 0, 0, tiled=True)]
    ppermute x0 -> x9, waiting for transfers between devices: none -> 17.4 us  [the longest x1 9.49 us: gather_group(): got[1, 1] = lax.ppermute(got[1, 0], 'x', down)]
  transfers between devices with their start and end apart: 5 -> 12, of which waited for: 4 -> 7; matrix products, arithmetic and copies ran while one was open for 2% -> 11% of each run, Pallas kernels for 0% -> 0%
where the time goes in v1:
time: 199 us; the launch traced here: 198 us
  starting transfers between devices  68.7 us (35%)
  waiting for transfers between devices  41.7 us (21%)
  matrix products  26.1 us (13%)
  other arithmetic  20.5 us (10%)
  between operations  18.3 us (9%)
  local copies, waits for them, and re-layouts  17.3 us (9%)
  blocking collectives  5.45 us (3%)
    all_to_all x1, starting transfers between devices, sum_over_groups(): tiles = lax.all_to_all(tiles, ('yh', 'z'), 0, 0, tiled=True)  21.7 us
    all_to_all x1, waiting for transfers between devices, sum_over_groups(): tiles = lax.all_to_all(tiles, ('yh', 'z'), 0, 0, tiled=True)  16.2 us
    ppermute x1, starting transfers between devices, gather_group(): got[1, 3] = lax.ppermute(got[0, 3], 'yl', flip)  9.76 us
    ppermute x1, waiting for transfers between devices, gather_group(): got[1, 1] = lax.ppermute(got[1, 0], 'x', down)  9.49 us
    dynamic_update_slice x8, local copies, waits for them, and re-layouts, body(): lax.dynamic_update_slice(all_features, block[:, width:width + depth], (pl...  8.93 us
    all_to_all x1, waiting for transfers between devices, sum_over_groups(): tiles = lax.all_to_all(send, ('yh', 'z'), 0, 0, tiled=True)  7.96 us
    dot_general x2, matrix products, right_product(): lax.dot_general(left, right, (((1,), (1,)), ((), ())), preferred_element_...  7.62 us
    dot_general x1, matrix products, compute(): du = 100.0 * jnp.dot(coupling, text_unit, preferred_element_type=F32)  7.22 us
  transfers between devices with their start and end apart: 12, of which 7 were waited for; matrix products, arithmetic and copies ran while one was open for 11% of the time, Pallas kernels for 0%

profile of v1, /device:TPU:1, one launch (start us, length us, event | category | flops | bytes accessed | tf_op | source)
XLA Modules:
  0.0 198.1 jit_solution(2519243428074239612)
XLA Ops:
  7.2 2.1 %fusion.14 = bf16[176,1920]{1,0:T(8,128)(2,1)} fusion(bf16[176,832]{1,0:T(8,128)(2,1)} %param.3, bf16[176,1024]{1,0:T(8,128)(2,1)} %param.5), kind=kLoop, calls=%fused_computation.30 | loop fusion | flops 2365440 | bytes 1329152 | tf_op jit(solution)/shard_map/concatenate | solution.py:159
  9.3 3.9 %collective-permute-start.1 = (bf16[176,1920]{1,0:T(8,128)(2,1)}, bf16[176,1920]{1,0:T(8,128)(2,1)}, u32[]{:S(2)}, u32[]{:S(2)}) collective-permute-start(bf16[176,1920]{1,0:T(8,128)(2,1)} %fusion.14), channel_id=1, source_target_pairs={{0,1},{1,2},{2,3},{3,0},{4,5},{5,6},{6,7},{7,4},{8,9},{9,10},{10,1... | collective-permute-start | bytes 2027528 | tf_op jit(solution)/shard_map/ppermute | solution.py:37
  13.2 3.2 %collective-permute-start = (bf16[176,1920]{1,0:T(8,128)(2,1)}, bf16[176,1920]{1,0:T(8,128)(2,1)}, u32[]{:S(2)}, u32[]{:S(2)}) collective-permute-start(bf16[176,1920]{1,0:T(8,128)(2,1)} %fusion.14), channel_id=1, source_target_pairs={{0,4},{4,0},{1,5},{5,1},{2,6},{6,2},{3,7},{7,3},{8,12},{12,8},{9,1... | collective-permute-start | bytes 2027528 | tf_op jit(solution)/shard_map/ppermute | solution.py:36
  16.4 3.4 %collective-permute-start.2 = (bf16[176,1920]{1,0:T(8,128)(2,1)}, bf16[176,1920]{1,0:T(8,128)(2,1)}, u32[]{:S(2)}, u32[]{:S(2)}) collective-permute-start(bf16[176,1920]{1,0:T(8,128)(2,1)} %fusion.14), channel_id=1, source_target_pairs={{0,3},{1,0},{2,1},{3,2},{4,7},{5,4},{6,5},{7,6},{8,11},{9,8},{10,9... | collective-permute-start | bytes 2027528 | tf_op jit(solution)/shard_map/ppermute | solution.py:38
  20.0 1.6 broadcast_in_dim.55
  21.6 0.7 constant_dynamic-update-slice_fusion.3
  23.0 9.8 %collective-permute-start.3 = (bf16[176,1920]{1,0:T(8,128)(2,1)}, bf16[176,1920]{1,0:T(8,128)(2,1)S(1)}, u32[]{:S(2)}, u32[]{:S(2)}) collective-permute-start(bf16[176,1920]{1,0:T(8,128)(2,1)} %collective-permute-done.1), channel_id=1, source_target_pairs={{0,4},{4,0},{1,5},{5,1},{2,6},{6,2},{3,7},{7,3},{8,12},{12,8},{9,1... | collective-permute-start | bytes 2027528 | tf_op jit(solution)/shard_map/ppermute | solution.py:39
  32.7 1.9 collective-permute-start.5
  34.7 4.6 %collective-permute-start.4 = (bf16[176,1920]{1,0:T(8,128)(2,1)}, bf16[176,1920]{1,0:T(8,128)(2,1)S(1)}, u32[]{:S(2)}, u32[]{:S(2)}) collective-permute-start(bf16[176,1920]{1,0:T(8,128)(2,1)} %collective-permute-done), channel_id=1, source_target_pairs={{0,3},{1,0},{2,1},{3,2},{4,7},{5,4},{6,5},{7,6},{8,11},{9,8},{10,9... | collective-permute-start | bytes 2027528 | tf_op jit(solution)/shard_map/ppermute | solution.py:40
  39.3 1.0 slice_dynamic-update-slice_fusion.6
  40.3 1.7 slice_dynamic-update-slice_fusion.13
  42.0 1.0 slice_dynamic-update-slice_fusion.5
  43.0 1.7 slice_dynamic-update-slice_fusion.12
  44.8 1.0 slice_dynamic-update-slice_fusion.4
  45.8 1.7 slice_dynamic-update-slice_fusion.11
  47.5 1.9 collective-permute-start.6
  49.5 9.5 %collective-permute-done.4 = bf16[176,1920]{1,0:T(8,128)(2,1)S(1)} collective-permute-done((bf16[176,1920]{1,0:T(8,128)(2,1)}, bf16[176,1920]{1,0:T(8,128)(2,1)S(1)}, u32[]{:S(2)}, u32[]{:S(2)}) %collective-permute-start.4) | collective-permute-done | bytes 675872 | tf_op jit(solution)/shard_map/ppermute | solution.py:40
  59.0 5.9 %collective-permute-start.7 = (bf16[96,1920]{1,0:T(8,128)(2,1)S(1)}, bf16[96,1920]{1,0:T(8,128)(2,1)S(1)}, u32[]{:S(2)}, u32[]{:S(2)}) collective-permute-start(bf16[96,1920]{1,0:T(8,128)(2,1)S(1)} %slice.118), channel_id=1, source_target_pairs={{0,3},{1,0},{2,1},{3,2},{4,7},{5,4},{6,5},{7,6},{8,11},{9,8},{10,9... | collective-permute-start | bytes 1105928 | tf_op jit(solution)/shard_map/ppermute | solution.py:43
  64.9 0.8 slice_dynamic-update-slice_fusion.10
  65.8 0.7 slice_dynamic-update-slice_fusion.9
  66.6 0.7 slice_dynamic-update-slice_fusion.8
  67.3 4.0 %collective-permute-done.6 = bf16[80,1920]{1,0:T(8,128)(2,1)S(1)} collective-permute-done((bf16[80,1920]{1,0:T(8,128)(2,1)S(1)}, bf16[80,1920]{1,0:T(8,128)(2,1)S(1)}, u32[]{:S(2)}, u32[]{:S(2)}) %collective-permute-start.6) | collective-permute-done | bytes 307232 | tf_op jit(solution)/shard_map/ppermute | solution.py:42
  71.3 2.8 %collective-permute-done.7 = bf16[96,1920]{1,0:T(8,128)(2,1)S(1)} collective-permute-done((bf16[96,1920]{1,0:T(8,128)(2,1)S(1)}, bf16[96,1920]{1,0:T(8,128)(2,1)S(1)}, u32[]{:S(2)}, u32[]{:S(2)}) %collective-permute-start.7) | collective-permute-done | bytes 368672 | tf_op jit(solution)/shard_map/ppermute | solution.py:43
  74.2 0.6 fusion
  74.8 0.8 slice_dynamic-update-slice_fusion.7
  75.6 5.5 %multiply_reduce_fusion.1 = (f32[1408]{0:T(1024)S(1)}, f32[1408,1024]{1,0:T(8,128)S(1)}) fusion(bf16[1408,832]{1,0:T(8,128)(2,1)} %slice_dynamic-update-slice_fusion.7, bf16[832,1024]{1,0:T(8,128)(2,1)} %all-gather.2.cloned.1.call-done), kind=kOutput, calls=%fused_computation.12 | convolution fusion | flops 2402023936 | bytes 9819648 | tf_op jit(solution)/shard_map/dot_general | solution.py:51
  81.1 5.1 %fusion.22 = (f32[1408]{0:T(1024)S(1)}, f32[1408]{0:T(1024)S(1)}, f32[1408,1408]{0,1:T(8,128)S(1)}) fusion(bf16[1408,1024]{1,0:T(8,128)(2,1)S(1)} %slice_dynamic-update-slice_fusion, f32[1408]{0:T(1024)S(1)} %add_rsqrt_fusion, f32[1408,1024]{1,0:T(8,128)S(1)} %get-tuple-element.16, f32[1408]{0:T(1024)S(1)} %add_rsqrt_fusion.1), kind=kOutput, calls=%fused_computation.91 | convolution fusion | flops 4073239552 | bytes 16603136 | tf_op jit(solution)/shard_map/dot_general | solution.py:17
  86.2 4.3 %exponential_reduce_fusion = (f32[1408]{0:T(1024)S(1)}, f32[1408]{0:T(1024)S(1)}, f32[1408]{0:T(1024)S(1)}) fusion(f32[1408,1408]{0,1:T(8,128)S(1)} %get-tuple-element.17, f32[1408]{0:T(1024)S(1)} %get-tuple-element.7, f32[1408]{0:T(1024)S(1)} %get-tuple-element.8), kind=kLoop, calls=%fused_computation.4 | loop fusion | flops 13873024 | bytes 7958016 | tf_op jit(solution)/shard_map/reduce_sum | solution.py:60
  90.5 0.6 subtract_reduce_fusion
  91.1 4.3 %subtract_convert_fusion = bf16[1408,1408]{0,1:T(8,128)(2,1)S(1)} fusion(f32[1408,1408]{0,1:T(8,128)S(1)} %get-tuple-element.17, f32[1408]{0:T(1024)S(1)} %get-tuple-element.12, f32[1408]{0:T(1024)S(1)} %get-tuple-element.11), kind=kLoop, calls=%fused_computation.2 | loop fusion | flops 13877248 | bytes 11906048 | tf_op jit(solution)/shard_map/convert_element_type | solution.py:71
  95.5 7.2 %multiply_reduce_fusion = (f32[1408]{0:T(1024)S(1)}, f32[1408,1024]{1,0:T(8,128)}) fusion(f32[1408,1024]{1,0:T(8,128)S(1)} %get-tuple-element.16, f32[1408]{0:T(1024)S(1)} %add_rsqrt_fusion.1, bf16[1408,1408]{0,1:T(8,128)(2,1)S(1)} %subtract_convert_fusion, bf16[1408,1024]{1,0:T(8,128)(2,1)S(1)} %slice_dynamic-update-slice_fusion, f32[1408]{0:T(1024)S(1)} %add_rsqrt_fusion), kind=kOutput, calls=%fused_computation.11 | convolution fusion | flops 4070177280 | bytes 18399744 | tf_op jit(solution)/shard_map/dot_general | solution.py:72
  104.0 5.0 %multiply_convert_fusion = bf16[1408,1024]{1,0:T(8,128)(2,1)S(1)} fusion(f32[1408,1024]{1,0:T(8,128)} %get-tuple-element.19, f32[1408,1024]{1,0:T(8,128)} %copy-done, f32[1408]{0:T(1024)S(1)} %get-tuple-element.18, f32[1408]{0:T(1024)S(1)} %add_rsqrt_fusion.1), kind=kLoop, calls=%fused_computation.10 | loop fusion | flops 8650752 | bytes 14429184 | tf_op jit(solution)/shard_map/convert_element_type | solution.py:73
  109.0 1.6 copy-done.1
  110.6 1.9 convolution_convert_fusion.1
  112.7 6.7 %collective-permute-start.8 = (bf16[128,512]{1,0:T(8,128)(2,1)S(1)}, bf16[128,512]{1,0:T(8,128)(2,1)S(1)}, u32[]{:S(2)}, u32[]{:S(2)}) collective-permute-start(bf16[128,512]{1,0:T(8,128)(2,1)S(1)} %pad_maximum_fusion), channel_id=1, source_target_pairs={{0,8},{8,0},{1,9},{9,1},{2,10},{10,2},{3,11},{11,3},{4,12},{12,4},... | collective-permute-start | bytes 393224 | tf_op jit(solution)/shard_map/ppermute | solution.py:114
  119.4 1.0 collective-permute-done.8
  121.8 0.7 pad.15
  122.5 21.7 %all-to-all-start = ((bf16[48,16,128]{2,1,0:T(8,128)(2,1)}), bf16[48,16,128]{2,1,0:T(8,128)(2,1)S(1)}, u32[]{:S(2)}, u32[]{:S(2)}) async-start(bf16[48,16,128]{2,1,0:T(8,128)(2,1)} %pad.15), calls=%async_computation | async-start | bytes 393216 | tf_op jit(solution)/shard_map/all_to_all | solution.py:125
  144.4 16.2 %all-to-all-done = bf16[48,16,128]{2,1,0:T(8,128)(2,1)S(1)} async-done(((bf16[48,16,128]{2,1,0:T(8,128)(2,1)}), bf16[48,16,128]{2,1,0:T(8,128)(2,1)S(1)}, u32[]{:S(2)}, u32[]{:S(2)}) %all-to-all-start) | async-done | bytes 196640 | tf_op jit(solution)/shard_map/all_to_all | solution.py:125
  160.8 0.7 reshape.147
  161.5 5.7 %all-to-all-start.1 = ((bf16[48,16,128]{2,1,0:T(8,128)(2,1)}), bf16[48,16,128]{2,1,0:T(8,128)(2,1)S(1)}, u32[]{:S(2)}, u32[]{:S(2)}) async-start(bf16[48,16,128]{2,1,0:T(8,128)(2,1)} %reshape.147), calls=%async_computation.1 | async-start | bytes 393216 | tf_op jit(solution)/shard_map/all_to_all | solution.py:136
  167.2 3.9 %fusion.9 = (f32[176]{0:T(256)S(1)}, f32[176,1024]{1,0:T(8,128)S(1)}) fusion(f32[176]{0:T(256)S(1)} %add_rsqrt_fusion.2, bf16[1408,1024]{1,0:T(8,128)(2,1)S(1)} %slice_dynamic-update-slice_fusion, s32[]{:T(128)S(6)} %select_n.163, f32[1408,1024]{1,0:T(8,128)} %copy-done, f32[1408]{0:T(1024)S(1)} %add_rsqrt_fusion.1, bf16[1408,1408]{0,1:T(8,128)(2,1)} %copy-done.2), kind=kOutput, calls=%fused_computation.25 | convolution fusion | flops 511295296 | bytes 7352192 | tf_op jit(solution)/shard_map/dot_general | solution.py:11
  171.1 1.0 fusion.12
  172.1 2.5 %convolution_convert_fusion = bf16[176,832]{1,0:T(8,128)(2,1)} fusion(bf16[832,1024]{1,0:T(8,128)(2,1)S(1)} %copy-done.3, bf16[1408,1024]{1,0:T(8,128)(2,1)} %copy-done.1, s32[]{:T(128)S(6)} %select_n.163), kind=kOutput, calls=%fused_computation.18 | convolution fusion | flops 300039168 | bytes 2357252 | tf_op jit(solution)/shard_map/dot_general | solution.py:17
  174.5 8.0 %all-to-all-done.1 = bf16[48,16,128]{2,1,0:T(8,128)(2,1)S(1)} async-done(((bf16[48,16,128]{2,1,0:T(8,128)(2,1)}), bf16[48,16,128]{2,1,0:T(8,128)(2,1)S(1)}, u32[]{:S(2)}, u32[]{:S(2)}) %all-to-all-start.1) | async-done | bytes 196640 | tf_op jit(solution)/shard_map/all_to_all | solution.py:136
  182.6 5.4 %all_gather.7 = bf16[112,1024]{1,0:T(8,128)(2,1)S(1)} all-gather(bf16[112,512]{1,0:T(8,128)(2,1)S(1)} %bitcast.26), channel_id=1, replica_groups=mesh['yh'=4,'z'=12,'core'=2,'yl'=2,'x'=4] {'core'}, dimensions={1}, use_global_device_ids=true | all-gather | bytes 344064 | tf_op jit(solution)/shard_map/all_gather | solution.py:140
  188.0 0.8 slice_convert_fusion
  188.8 0.6 convert_reduce_fusion.1
  (53 shorter events, 2.3 us)
Async XLA Ops:
  7.2 14.4 %copy-start.5 = (bf16[176,832]{1,0:T(8,128)(2,1)S(1)}, bf16[176,832]{1,0:T(8,128)(2,1)}, u32[]{:S(2)}) copy-start(bf16[176,832]{1,0:T(8,128)(2,1)} %param.3) | copy-start | bytes 878596
  7.2 68.4 %all-gather.2.cloned.1.call-start = ((), (), s32[]{:S(2)}) async-start(), calls=%async_computation.2 | async-start | bytes 1916928 | tf_op jit(solution)/shard_map/all_gather | solution.py:158
  9.3 13.7 %collective-permute-start.1 = (bf16[176,1920]{1,0:T(8,128)(2,1)}, bf16[176,1920]{1,0:T(8,128)(2,1)}, u32[]{:S(2)}, u32[]{:S(2)}) collective-permute-start(bf16[176,1920]{1,0:T(8,128)(2,1)} %fusion.14), channel_id=1, source_target_pairs={{0,1},{1,2},{2,3},{3,0},{4,5},{5,6},{6,7},{7,4},{8,9},{9,10},{10,1... | collective-permute-start | bytes 2027528 | tf_op jit(solution)/shard_map/ppermute | solution.py:37
  13.2 21.5 %collective-permute-start = (bf16[176,1920]{1,0:T(8,128)(2,1)}, bf16[176,1920]{1,0:T(8,128)(2,1)}, u32[]{:S(2)}, u32[]{:S(2)}) collective-permute-start(bf16[176,1920]{1,0:T(8,128)(2,1)} %fusion.14), channel_id=1, source_target_pairs={{0,4},{4,0},{1,5},{5,1},{2,6},{6,2},{3,7},{7,3},{8,12},{12,8},{9,1... | collective-permute-start | bytes 2027528 | tf_op jit(solution)/shard_map/ppermute | solution.py:36
  16.4 28.3 %collective-permute-start.2 = (bf16[176,1920]{1,0:T(8,128)(2,1)}, bf16[176,1920]{1,0:T(8,128)(2,1)}, u32[]{:S(2)}, u32[]{:S(2)}) collective-permute-start(bf16[176,1920]{1,0:T(8,128)(2,1)} %fusion.14), channel_id=1, source_target_pairs={{0,3},{1,0},{2,1},{3,2},{4,7},{5,4},{6,5},{7,6},{8,11},{9,8},{10,9... | collective-permute-start | bytes 2027528 | tf_op jit(solution)/shard_map/ppermute | solution.py:38
  20.0 2.7 %copy-start.4 = (bf16[176,1024]{1,0:T(8,128)(2,1)S(1)}, bf16[176,1024]{1,0:T(8,128)(2,1)}, u32[]{:S(2)}) copy-start(bf16[176,1024]{1,0:T(8,128)(2,1)} %param.5) | copy-start | bytes 1081348
  23.0 24.5 %collective-permute-start.3 = (bf16[176,1920]{1,0:T(8,128)(2,1)}, bf16[176,1920]{1,0:T(8,128)(2,1)S(1)}, u32[]{:S(2)}, u32[]{:S(2)}) collective-permute-start(bf16[176,1920]{1,0:T(8,128)(2,1)} %collective-permute-done.1), channel_id=1, source_target_pairs={{0,4},{4,0},{1,5},{5,1},{2,6},{6,2},{3,7},{7,3},{8,12},{12,8},{9,1... | collective-permute-start | bytes 2027528 | tf_op jit(solution)/shard_map/ppermute | solution.py:39
  32.7 33.0 %collective-permute-start.5 = (bf16[176,1920]{1,0:T(8,128)(2,1)}, bf16[176,1920]{1,0:T(8,128)(2,1)S(1)}, u32[]{:S(2)}, u32[]{:S(2)}) collective-permute-start(bf16[176,1920]{1,0:T(8,128)(2,1)} %collective-permute-done.1), channel_id=1, source_target_pairs={{0,1},{1,2},{2,3},{3,0},{4,5},{5,6},{6,7},{7,4},{8,9},{9,10},{10,1... | collective-permute-start | bytes 2027528 | tf_op jit(solution)/shard_map/ppermute | solution.py:41
  34.7 24.3 %collective-permute-start.4 = (bf16[176,1920]{1,0:T(8,128)(2,1)}, bf16[176,1920]{1,0:T(8,128)(2,1)S(1)}, u32[]{:S(2)}, u32[]{:S(2)}) collective-permute-start(bf16[176,1920]{1,0:T(8,128)(2,1)} %collective-permute-done), channel_id=1, source_target_pairs={{0,3},{1,0},{2,1},{3,2},{4,7},{5,4},{6,5},{7,6},{8,11},{9,8},{10,9... | collective-permute-start | bytes 2027528 | tf_op jit(solution)/shard_map/ppermute | solution.py:40
  47.5 23.8 %collective-permute-start.6 = (bf16[80,1920]{1,0:T(8,128)(2,1)S(1)}, bf16[80,1920]{1,0:T(8,128)(2,1)S(1)}, u32[]{:S(2)}, u32[]{:S(2)}) collective-permute-start(bf16[80,1920]{1,0:T(8,128)(2,1)S(1)} %slice.117), channel_id=1, source_target_pairs={{0,1},{1,2},{2,3},{3,0},{4,5},{5,6},{6,7},{7,4},{8,9},{9,10},{10,1... | collective-permute-start | bytes 921608 | tf_op jit(solution)/shard_map/ppermute | solution.py:42
  59.0 15.1 %collective-permute-start.7 = (bf16[96,1920]{1,0:T(8,128)(2,1)S(1)}, bf16[96,1920]{1,0:T(8,128)(2,1)S(1)}, u32[]{:S(2)}, u32[]{:S(2)}) collective-permute-start(bf16[96,1920]{1,0:T(8,128)(2,1)S(1)} %slice.118), channel_id=1, source_target_pairs={{0,3},{1,0},{2,1},{3,2},{4,7},{5,4},{6,5},{7,6},{8,11},{9,8},{10,9... | collective-permute-start | bytes 1105928 | tf_op jit(solution)/shard_map/ppermute | solution.py:43
  81.1 14.4 %copy-start = (f32[1408,1024]{1,0:T(8,128)}, f32[1408,1024]{1,0:T(8,128)S(1)}, u32[]{:S(2)}) copy-start(f32[1408,1024]{1,0:T(8,128)S(1)} %get-tuple-element.16) | copy-start | bytes 17301508
  95.5 7.2 %copy-start.2 = (bf16[1408,1408]{0,1:T(8,128)(2,1)}, bf16[1408,1408]{0,1:T(8,128)(2,1)S(1)}, u32[]{:S(2)}) copy-start(bf16[1408,1408]{0,1:T(8,128)(2,1)S(1)} %subtract_convert_fusion) | copy-start | bytes 11894788
  109.0 1.6 copy-start.1
  112.7 7.6 %collective-permute-start.8 = (bf16[128,512]{1,0:T(8,128)(2,1)S(1)}, bf16[128,512]{1,0:T(8,128)(2,1)S(1)}, u32[]{:S(2)}, u32[]{:S(2)}) collective-permute-start(bf16[128,512]{1,0:T(8,128)(2,1)S(1)} %pad_maximum_fusion), channel_id=1, source_target_pairs={{0,8},{8,0},{1,9},{9,1},{2,10},{10,2},{3,11},{11,3},{4,12},{12,4},... | collective-permute-start | bytes 393224 | tf_op jit(solution)/shard_map/ppermute | solution.py:114
  122.5 38.1 %all-to-all-start = ((bf16[48,16,128]{2,1,0:T(8,128)(2,1)}), bf16[48,16,128]{2,1,0:T(8,128)(2,1)S(1)}, u32[]{:S(2)}, u32[]{:S(2)}) async-start(bf16[48,16,128]{2,1,0:T(8,128)(2,1)} %pad.15), calls=%async_computation | async-start | bytes 393216 | tf_op jit(solution)/shard_map/all_to_all | solution.py:125
  161.5 21.0 %all-to-all-start.1 = ((bf16[48,16,128]{2,1,0:T(8,128)(2,1)}), bf16[48,16,128]{2,1,0:T(8,128)(2,1)S(1)}, u32[]{:S(2)}, u32[]{:S(2)}) async-start(bf16[48,16,128]{2,1,0:T(8,128)(2,1)} %reshape.147), calls=%async_computation.1 | async-start | bytes 393216 | tf_op jit(solution)/shard_map/all_to_all | solution.py:136
  167.2 4.9 %copy-start.3 = (bf16[832,1024]{1,0:T(8,128)(2,1)S(1)}, bf16[832,1024]{1,0:T(8,128)(2,1)}, u32[]{:S(2)}) copy-start(bf16[832,1024]{1,0:T(8,128)(2,1)} %all-gather.2.cloned.1.call-done) | copy-start | bytes 5111812
Sparse Core Ops, SparseCore 0:
  20.0 54.4 all-gather.1

commit v2 on v1

v2 whole, which is shorter than its diff:
```python
import functools

import jax
import jax.numpy as jnp
from jax import lax
from jax.experimental import pallas as pl
from jax.experimental.pallas import tpu as pltpu
from jax.sharding import Mesh, PartitionSpec as P

BF = jnp.bfloat16
F32 = jnp.float32
LOG2E = 1.4426950408889634
LN2 = 0.6931471805599453
CHUNK = 128
NT = (((1,), (1,)), ((), ()))
TN = (((0,), (0,)), ((), ()))


def spans(size, step):
    return [(at, min(step, size - at)) for at in range(0, size, step)]


def group_kernel(n_fs, depth, place_ref, weight_ref, *refs):
    blocks = refs[: n_fs + 1]
    head_ref, loss_ref, unit_out, coupling_out, dz_out = refs[n_fs + 1 : n_fs + 6]
    packed, weight, u_full, inv_u, unit, text, score, prob, coupling, dz, dg, sems, wsem, osem = refs[n_fs + 6 :]
    group, width = unit.shape
    rows = group // n_fs
    padded = weight.shape[0]
    own = place_ref[0]
    copies = []
    for k in range(n_fs - 1):
        at = pl.multiple_of(place_ref[k] * rows, 16)
        copies.append(pltpu.make_async_copy(blocks[k], packed.at[pl.ds(at, rows)], sems.at[k]))
    cut = blocks[n_fs - 1].shape[0]
    at = pl.multiple_of(place_ref[n_fs - 1] * rows, 16)
    copies.append(pltpu.make_async_copy(blocks[n_fs - 1], packed.at[pl.ds(at, cut)], sems.at[n_fs - 1]))
    copies.append(pltpu.make_async_copy(blocks[n_fs], packed.at[pl.ds(at + cut, rows - cut)], sems.at[n_fs]))
    copies.append(pltpu.make_async_copy(weight_ref, weight.at[pl.ds(0, depth)], wsem))
    for copy in copies:
        copy.start()
    weight[depth:, :] = jnp.zeros((padded - depth, width), BF)
    dg[...] = jnp.zeros_like(dg)
    for copy in copies:
        copy.wait()

    for at, size in spans(width, 256):
        u_full[:, at : at + size] = jnp.dot(
            packed[:, width:], weight[:, at : at + size], preferred_element_type=F32
        )

    def normalise(k, carry):
        r = pl.ds(pl.multiple_of(k * CHUNK, CHUNK), CHUNK)
        z = u_full[r, :]
        inverse = lax.rsqrt(jnp.sum(z * z, axis=1, keepdims=True) + 1e-06)
        u = z * inverse
        u_full[r, :] = u
        unit[r, :] = u.astype(BF)
        inv_u[r, :] = jnp.broadcast_to(inverse, (CHUNK, 128))
        t = packed[r, :width].astype(F32)
        inverse = lax.rsqrt(jnp.sum(t * t, axis=1, keepdims=True) + 1e-06)
        text[r, :] = (t * inverse).astype(BF)
        return carry

    lax.fori_loop(0, group // CHUNK, normalise, 0)
    out_unit = pltpu.make_async_copy(unit, unit_out, osem.at[0])
    out_unit.start()

    for at, size in spans(group, 256):
        score[:, at : at + size] = lax.dot_general(
            unit[...], text[at : at + size, :], NT, preferred_element_type=F32
        )

    lane = lax.broadcasted_iota(jnp.int32, (CHUNK, 128), 1)
    line = lax.broadcasted_iota(jnp.int32, (CHUNK, 128), 0)

    def window(k):
        at = k * CHUNK
        left = at // 128 * 128
        return pl.ds(pl.multiple_of(left, 128), 128), (lane - line) == (at - left)

    def tiles(values):
        return values.reshape(CHUNK // 8, 8, values.shape[1])

    def by_row(k, carry):
        peak, terms = carry
        r = pl.ds(pl.multiple_of(k * CHUNK, CHUNK), CHUNK)
        s = score[r, :] * (100.0 * LOG2E)
        score[r, :] = s
        m = jnp.max(s, axis=1, keepdims=True)
        p = jnp.exp2(s - m)
        total = jnp.sum(p, axis=1, keepdims=True)
        prob[r, :] = p * (1.0 / total)
        cols, eye = window(k)
        diagonal = jnp.where(eye, score[r, cols], 0.0)
        dg[:, cols] += jnp.sum(tiles(diagonal), axis=0)
        term = m + jnp.log2(total) - jnp.sum(diagonal, axis=1, keepdims=True)
        return jnp.maximum(peak, jnp.max(tiles(s), axis=0)), terms + term

    peak, row_terms = lax.fori_loop(
        0,
        group // CHUNK,
        by_row,
        (jnp.full((8, group), -jnp.inf, F32), jnp.zeros((CHUNK, 1), F32)),
    )
    peak = jnp.max(peak, axis=0, keepdims=True)

    def by_col(k, total):
        r = pl.ds(pl.multiple_of(k * CHUNK, CHUNK), CHUNK)
        q = jnp.exp2(score[r, :] - peak)
        score[r, :] = q
        return total + jnp.sum(tiles(q), axis=0)

    total = lax.fori_loop(0, group // CHUNK, by_col, jnp.zeros((8, group), F32))
    total = jnp.sum(total, axis=0, keepdims=True)
    col_terms = peak + jnp.log2(total) - jnp.sum(dg[...], axis=0, keepdims=True)
    loss = LN2 * (jnp.sum(row_terms) + jnp.sum(col_terms))
    loss_ref[...] = jnp.full(loss_ref.shape, loss, F32)
    dg[0:1, :] = 1.0 / total

    def couple(k, carry):
        r = pl.ds(pl.multiple_of(k * CHUNK, CHUNK), CHUNK)
        coupling[r, :] = (prob[r, :] + score[r, :] * dg[0:1, :]).astype(BF)
        cols, eye = window(k)
        c = prob[r, cols] + score[r, cols] * dg[0:1, cols]
        coupling[r, cols] = (c - jnp.where(eye, 2.0, 0.0)).astype(BF)
        return carry

    lax.fori_loop(0, group // CHUNK, couple, 0)
    out_coupling = pltpu.make_async_copy(coupling, coupling_out, osem.at[1])
    out_coupling.start()

    for at, size in spans(width, 256):
        prob[:, at : at + size] = jnp.dot(
            coupling[...], text[:, at : at + size], preferred_element_type=F32
        )

    def to_dz(k, carry):
        r = pl.ds(pl.multiple_of(k * CHUNK, CHUNK), CHUNK)
        du = 100.0 * prob[r, :width]
        u = u_full[r, :]
        along = jnp.sum(u * du, axis=1, keepdims=True)
        dz[r, :] = ((du - u * along) * inv_u[r, 0:1]).astype(BF)
        return carry

    lax.fori_loop(0, group // CHUNK, to_dz, 0)
    mine = dz.at[pl.ds(pl.multiple_of(own * rows, 16), rows)]
    out_dz = pltpu.make_async_copy(mine, dz_out, osem.at[2])
    out_dz.start()

    columns = depth // n_fs
    pick = (
        lax.broadcasted_iota(jnp.int32, (padded, 128), 0)
        == own * columns + lax.broadcasted_iota(jnp.int32, (padded, 128), 1)
    ) & (lax.broadcasted_iota(jnp.int32, (padded, 128), 1) < columns)
    features = jnp.dot(
        packed[:, width:], pick.astype(F32).astype(BF), preferred_element_type=F32
    ).astype(BF)
    head = lax.dot_general(features, dz[...], TN, preferred_element_type=F32)
    head_ref[...] = head[: head_ref.shape[0], :].astype(BF)
    out_unit.wait()
    out_coupling.wait()
    out_dz.wait()


def group_call(place, weight, blocks, depth):
    n_fs = len(blocks) - 1
    rows, lanes = blocks[0].shape
    width = weight.shape[1]
    group = n_fs * rows
    padded = lanes - width
    head_rows = -(-(depth // n_fs) // 16) * 16
    anywhere = pl.BlockSpec(memory_space=pl.ANY)
    inside = pl.BlockSpec(memory_space=pltpu.VMEM)
    return pl.pallas_call(
        functools.partial(group_kernel, n_fs, depth),
        out_shape=(
            jax.ShapeDtypeStruct((head_rows, width), BF),
            jax.ShapeDtypeStruct((8, 128), F32),
            jax.ShapeDtypeStruct((group, width), BF),
            jax.ShapeDtypeStruct((group, group), BF),
            jax.ShapeDtypeStruct((rows, width), BF),
        ),
        in_specs=[pl.BlockSpec(memory_space=pltpu.SMEM)] + [anywhere] * (len(blocks) + 1),
        out_specs=(inside, inside, anywhere, anywhere, anywhere),
        scratch_shapes=[
            pltpu.VMEM((group, lanes), BF),
            pltpu.VMEM((padded, width), BF),
            pltpu.VMEM((group, width), F32),
            pltpu.VMEM((group, 128), F32),
            pltpu.VMEM((group, width), BF),
            pltpu.VMEM((group, width), BF),
            pltpu.VMEM((group, group), F32),
            pltpu.VMEM((group, group), F32),
            pltpu.VMEM((group, group), BF),
            pltpu.VMEM((group, width), BF),
            pltpu.VMEM((8, group), F32),
            pltpu.SemaphoreType.DMA((n_fs + 1,)),
            pltpu.SemaphoreType.DMA,
            pltpu.SemaphoreType.DMA((3,)),
        ],
        compiler_params=pltpu.CompilerParams(vmem_limit_bytes=60 * 1024 * 1024),
        cost_estimate=pl.CostEstimate(
            flops=12 * 10**9, bytes_accessed=20 * 10**6, transcendentals=4 * 10**6
        ),
        name="group",
    )(place, weight, *blocks)


def left_product(left, right):
    return lax.dot_general(
        left, right, (((0,), (0,)), ((), ())), preferred_element_type=F32
    )


def right_product(left, right):
    return lax.dot_general(
        left, right, (((1,), (1,)), ((), ())), preferred_element_type=F32
    )


def unit_rows(vectors):
    inverse = lax.rsqrt(jnp.sum(vectors * vectors, axis=-1, keepdims=True) + 1e-06)
    return (vectors * inverse, inverse)


def ring(size, step):
    return [(i, (i + step) % size) for i in range(size)]


def gather_group(block, n_y, n_x):
    flip, up, down = ring(n_y, 1), ring(n_x, 1), ring(n_x, -1)
    rows = block.shape[0]
    half = rows // 2 // 16 * 16
    got = {(0, 0): block}
    got[1, 0] = lax.ppermute(block, "yl", flip)
    got[0, 3] = lax.ppermute(block, "x", up)
    got[0, 1] = lax.ppermute(block, "x", down)
    got[1, 3] = lax.ppermute(got[0, 3], "yl", flip)
    got[1, 1] = lax.ppermute(got[1, 0], "x", down)
    got[0, 2] = lax.ppermute(got[0, 3], "x", up)
    low = lax.ppermute(got[1, 3][:half], "x", up)
    high = lax.ppermute(got[1, 1][half:], "x", down)
    keys = list(got) + [(1, 2)]
    return keys, list(got.values()) + [low, high]


def gather_head(head_weight, part, n_fs):
    rows, width = head_weight.shape
    half = width // 2
    core = lax.axis_index("core")
    mine = jnp.where(core == 0, head_weight[:, :half], head_weight[:, half:])
    mine = jnp.broadcast_to(mine[None], (n_fs, rows, half))
    mine = lax.all_to_all(mine, part, 0, 0, tiled=True).reshape(n_fs * rows, half)
    other = lax.ppermute(mine, "core", [(0, 1), (1, 0)])
    left = jnp.where(core == 0, mine, other)
    right = jnp.where(core == 0, other, mine)
    return jnp.concatenate([left, right], axis=1)


def pieces(value):
    one = value.astype(BF)
    two = (value - one.astype(F32)).astype(BF)
    three = (value - one.astype(F32) - two.astype(F32)).astype(BF)
    return one, two, three


def loss_rows(loss, width):
    lane = lax.broadcasted_iota(jnp.int32, (16, width), 1)
    row = lax.broadcasted_iota(jnp.int32, (16, width), 0)
    out = jnp.zeros((16, width), BF)
    for k, piece in enumerate(pieces(loss)):
        out = jnp.where((lane == k) & (row == 0), piece, out)
    return out


def sum_over_groups(head, loss, n_h, n_z):
    padded, width = head.shape
    core = lax.axis_index("core")
    half = width // 2
    first, second = head[:, :half], head[:, half:]
    tail = loss_rows(loss, half)
    mine = jnp.where(core == 0, first, second)
    other = jnp.where(core == 0, second, first)
    other = jnp.concatenate([other, tail], axis=0)
    came = lax.ppermute(other, "core", [(0, 1), (1, 0)])
    both = (mine.astype(F32) + came[:padded].astype(F32)).astype(BF)
    chip_loss = loss + jnp.sum(came[padded].astype(F32)[:3])
    both = jnp.concatenate([both, loss_rows(chip_loss, half)], axis=0)
    lanes = half // 128
    groups = both.shape[0] // 16
    tiles = both.reshape(groups, 16, lanes, 128).transpose(0, 2, 1, 3).reshape(-1, 16, 128)
    peers = n_h * n_z
    count = tiles.shape[0]
    each = -(-count // peers)
    tiles = jnp.pad(tiles, ((0, each * peers - count), (0, 0), (0, 0)))
    tiles = lax.all_to_all(tiles, ("yh", "z"), 0, 0, tiled=True)
    total = jnp.sum(tiles.reshape(peers, each, 16, 128).astype(F32), axis=0)
    loss_tile = count - lanes
    place = (lax.axis_index("yh") * n_z + lax.axis_index("z")) * each
    here = (place + lax.broadcasted_iota(jnp.int32, (each, 16, 128), 0)) == loss_tile
    row = lax.broadcasted_iota(jnp.int32, (each, 16, 128), 1)
    one, two, three = pieces(total[:, :1])
    send = total.astype(BF)
    send = jnp.where(here & (row == 1), two, send)
    send = jnp.where(here & (row == 2), three, send)
    send = jnp.broadcast_to(send[None], (peers, each, 16, 128)).reshape(-1, 16, 128)
    tiles = lax.all_to_all(send, ("yh", "z"), 0, 0, tiled=True)
    loss = jnp.sum(tiles[loss_tile][:3, :3].astype(F32))
    tiles = tiles[: (padded // 16) * lanes].reshape(padded // 16, lanes, 16, 128)
    part = tiles.transpose(0, 2, 1, 3).reshape(padded, half)
    whole = lax.all_gather(part, "core", axis=1, tiled=True)
    return whole.astype(F32), loss


def solution(mesh):
    n_dp, n_fs = mesh.devices.shape
    n_x, n_y = 4, 2
    n_h = 4 if n_dp % 8 == 0 else 1
    n_z = n_dp // (2 * n_h)
    fine = Mesh(
        mesh.devices.reshape(n_h, n_z, 2, n_y, n_x), ("yh", "z", "core", "yl", "x")
    )
    every = ("yh", "z", "core", "yl", "x")
    part = ("yl", "x")

    def body(features, head_weight, text_embed):
        rows, depth = features.shape
        width = text_embed.shape[1]
        weight = gather_head(head_weight, part, n_fs)
        packed = jnp.concatenate([text_embed, features], axis=1)
        packed = jnp.pad(packed, ((0, 0), (0, -packed.shape[1] % 128)))
        keys, blocks = gather_group(packed, n_y, n_x)
        y, x = lax.axis_index("yl"), lax.axis_index("x")
        place = jnp.stack(
            [((y + dy) % n_y) * n_x + (x + dx) % n_x for dy, dx in keys]
        ).astype(jnp.int32)
        head, loss, image_unit, coupling, dz = group_call(place, weight, blocks, depth)
        own_coupling = lax.dynamic_slice(
            coupling, (0, place[0] * rows), (n_fs * rows, rows)
        )
        dv = 100.0 * left_product(own_coupling, image_unit)
        v_rows, inv_v = unit_rows(text_embed.astype(F32))
        text_grad = (
            (dv - v_rows * jnp.sum(v_rows * dv, axis=-1, keepdims=True)) * inv_v
        ).astype(BF)
        feat_grad = right_product(dz, weight).astype(BF)
        head_grad, loss = sum_over_groups(head, loss[0, 0], n_h, n_z)
        head_grad = head_grad[: head_weight.shape[0]]
        loss = loss / (2.0 * n_fs * rows * n_dp)
        return (loss, feat_grad, text_grad, head_grad)

    in_specs = (P(every, None), P(part, None), P(every, None))
    out_specs = (P(), P(every, None), P(every, None), P(part, None))
    return jax.shard_map(
        body, mesh=fine, in_specs=in_specs, out_specs=out_specs, check_vma=False
    )
```

time: 199 us -> 189 us (0.950)
  Pallas kernels: 0 us -> 28.8 us
  matrix products: 26.1 us -> 4.79 us
  starting transfers between devices: 68.7 us -> 84.4 us
  between operations: 18.3 us -> 5.45 us
  local copies, waits for them, and re-layouts: 17.3 us -> 5.78 us
  other arithmetic: 20.5 us -> 10.3 us
    pallas_call x0 -> x1, Pallas kernels: none -> 28.8 us  [group_call(): pl.pallas_call(functools.partial(group_kernel, n_fs, depth), out_shape=(j...]
    ppermute x0 -> x1, starting transfers between devices: none -> 14.3 us  [gather_head(): other = lax.ppermute(mine, 'core', [(0, 1), (1, 0)])]
    dot_general x2 -> x0, matrix products: 12.7 us -> none  [the longest x1 7.22 us: compute(): du = 100.0 * jnp.dot(coupling, text_unit, preferred_element_type=F32)]
    dynamic_update_slice x16 -> x0, local copies, waits for them, and re-layouts: 12.1 us -> none  [the longest x8 8.93 us: body(): lax.dynamic_update_slice(all_features, block[:, width:width + depth], (pl...]
    convert_element_type x4 -> x1, other arithmetic: 11.1 us -> 0.98 us  [body(): text_grad = ((dv - v_rows * jnp.sum(v_rows * dv, axis=-1, keepdims=True))...]
    ppermute x1, waiting for transfers between devices: 9.49 us -> 0.01 us  [gather_group(): got[1, 1] = lax.ppermute(got[1, 0], 'x', down)]
    ppermute x1, starting transfers between devices: 9.76 us -> 2.65 us  [gather_group(): got[1, 3] = lax.ppermute(got[0, 3], 'yl', flip)]
    ppermute x1, waiting for transfers between devices: 0.01 us -> 6.39 us  [gather_group(): got[0, 1] = lax.ppermute(block, 'x', down)]
  transfers between devices with their start and end apart: 12 -> 13, of which waited for: 7 -> 8; matrix products, arithmetic and copies ran while one was open for 11% -> 6% of each run, Pallas kernels for 0% -> 0%
where the time goes in v2:
time: 189 us; the launch traced here: 188 us
  starting transfers between devices  84.4 us (45%)
  waiting for transfers between devices  43.1 us (23%)
  Pallas kernels  28.8 us (15%)
  other arithmetic  10.3 us (5%)
  local copies, waits for them, and re-layouts  5.78 us (3%)
  between operations  5.45 us (3%)
  blocking collectives  5.32 us (3%)
  matrix products  4.79 us (3%)
    pallas_call x1, Pallas kernels, group_call(): pl.pallas_call(functools.partial(group_kernel, n_fs, depth), out_shape=(j...  28.8 us
    all_to_all x1, starting transfers between devices, sum_over_groups(): tiles = lax.all_to_all(tiles, ('yh', 'z'), 0, 0, tiled=True)  24.9 us
    all_to_all x1, waiting for transfers between devices, sum_over_groups(): tiles = lax.all_to_all(tiles, ('yh', 'z'), 0, 0, tiled=True)  14.7 us
    ppermute x1, starting transfers between devices, gather_head(): other = lax.ppermute(mine, 'core', [(0, 1), (1, 0)])  14.3 us
    all_to_all x1, waiting for transfers between devices, sum_over_groups(): tiles = lax.all_to_all(send, ('yh', 'z'), 0, 0, tiled=True)  11.2 us
    ppermute x1, starting transfers between devices, sum_over_groups(): came = lax.ppermute(other, 'core', [(0, 1), (1, 0)])  7.77 us
    ppermute x1, waiting for transfers between devices, gather_group(): high = lax.ppermute(got[1, 1][half:], 'x', down)  6.87 us
    ppermute x1, waiting for transfers between devices, gather_group(): got[0, 1] = lax.ppermute(block, 'x', down)  6.39 us
  transfers between devices with their start and end apart: 13, of which 8 were waited for; matrix products, arithmetic and copies ran while one was open for 6% of the time, Pallas kernels for 0%

profile of v2, /device:TPU:1, one launch (start us, length us, event | category | flops | bytes accessed | tf_op | source)
XLA Modules:
  0.0 187.9 jit_solution(4884213437449764811)
XLA Ops:
  0.7 1.0 slice_select_fusion
  1.7 1.0 broadcast_in_dim.48
  2.6 5.9 %all-to-all-start = ((bf16[8,104,512]{2,1,0:T(8,128)(2,1)}), bf16[8,104,512]{2,1,0:T(8,128)(2,1)S(1)}, u32[]{:S(2)}, u32[]{:S(2)}) async-start(bf16[8,104,512]{2,1,0:T(8,128)(2,1)} %broadcast_in_dim.48), calls=%async_computation | async-start | bytes 1703936 | tf_op jit(solution)/shard_map/all_to_all | solution.py:254
  8.5 1.0 fusion.10.refs_0_
  9.5 3.4 %collective-permute-start.2 = (bf16[176,1920]{1,0:T(8,128)(2,1)}, bf16[176,1920]{1,0:T(8,128)(2,1)}, u32[]{:S(2)}, u32[]{:S(2)}) collective-permute-start(bf16[176,1920]{1,0:T(8,128)(2,1)} %fusion.10.refs_0_), channel_id=1, source_target_pairs={{0,1},{1,2},{2,3},{3,0},{4,5},{5,6},{6,7},{7,4},{8,9},{9,10},{10,1... | collective-permute-start | bytes 2027528 | tf_op jit(solution)/shard_map/ppermute | solution.py:237
  12.9 3.1 %collective-permute-start.1 = (bf16[176,1920]{1,0:T(8,128)(2,1)}, bf16[176,1920]{1,0:T(8,128)(2,1)}, u32[]{:S(2)}, u32[]{:S(2)}) collective-permute-start(bf16[176,1920]{1,0:T(8,128)(2,1)} %fusion.10.refs_0_), channel_id=1, source_target_pairs={{0,4},{4,0},{1,5},{5,1},{2,6},{6,2},{3,7},{7,3},{8,12},{12,8},{9,1... | collective-permute-start | bytes 2027528 | tf_op jit(solution)/shard_map/ppermute | solution.py:236
  16.0 1.2 all-to-all-done
  17.1 14.3 %collective-permute-start = (bf16[832,512]{1,0:T(8,128)(2,1)S(1)}, bf16[832,512]{1,0:T(8,128)(2,1)}, u32[]{:S(2)}, u32[]{:S(2)}) collective-permute-start(bf16[832,512]{1,0:T(8,128)(2,1)S(1)} %bitcast.32), channel_id=1, source_target_pairs={{0,8},{8,0},{1,9},{9,1},{2,10},{10,2},{3,11},{11,3},{4,12},{12,4},... | collective-permute-start | bytes 2555912 | tf_op jit(solution)/shard_map/ppermute | solution.py:255
  31.5 0.0 collective-permute-done.2.refs_2_
  31.5 2.7 %collective-permute-start.4 = (bf16[176,1920]{1,0:T(8,128)(2,1)}, bf16[176,1920]{1,0:T(8,128)(2,1)S(1)}, u32[]{:S(2)}, u32[]{:S(2)}) collective-permute-start(bf16[176,1920]{1,0:T(8,128)(2,1)} %collective-permute-done.2.refs_2_), channel_id=1, source_target_pairs={{0,4},{4,0},{1,5},{5,1},{2,6},{6,2},{3,7},{7,3},{8,12},{12,8},{9,1... | collective-permute-start | bytes 2027528 | tf_op jit(solution)/shard_map/ppermute | solution.py:239
  34.2 3.8 %collective-permute-start.5 = (bf16[176,1920]{1,0:T(8,128)(2,1)}, bf16[176,1920]{1,0:T(8,128)(2,1)S(1)}, u32[]{:S(2)}, u32[]{:S(2)}) collective-permute-start(bf16[176,1920]{1,0:T(8,128)(2,1)} %collective-permute-done.1.refs_1_), channel_id=1, source_target_pairs={{0,3},{1,0},{2,1},{3,2},{4,7},{5,4},{6,5},{7,6},{8,11},{9,8},{10,9... | collective-permute-start | bytes 2027528 | tf_op jit(solution)/shard_map/ppermute | solution.py:240
  38.0 2.5 %collective-permute-start.3 = (bf16[176,1920]{1,0:T(8,128)(2,1)}, bf16[176,1920]{1,0:T(8,128)(2,1)}, u32[]{:S(2)}, u32[]{:S(2)}) collective-permute-start(bf16[176,1920]{1,0:T(8,128)(2,1)} %fusion.10.refs_0_), channel_id=1, source_target_pairs={{0,3},{1,0},{2,1},{3,2},{4,7},{5,4},{6,5},{7,6},{8,11},{9,8},{10,9... | collective-permute-start | bytes 2027528 | tf_op jit(solution)/shard_map/ppermute | solution.py:238
  40.6 0.7 stack.35.place_ref
  41.3 2.8 %collective-permute-start.6 = (bf16[176,1920]{1,0:T(8,128)(2,1)}, bf16[176,1920]{1,0:T(8,128)(2,1)S(1)}, u32[]{:S(2)}, u32[]{:S(2)}) collective-permute-start(bf16[176,1920]{1,0:T(8,128)(2,1)} %collective-permute-done.2.refs_2_), channel_id=1, source_target_pairs={{0,1},{1,2},{2,3},{3,0},{4,5},{5,6},{6,7},{7,4},{8,9},{9,10},{10,1... | collective-permute-start | bytes 2027528 | tf_op jit(solution)/shard_map/ppermute | solution.py:241
  44.1 1.6 collective-permute-done.4.refs_4_
  45.7 5.6 %collective-permute-start.7 = (bf16[80,1920]{1,0:T(8,128)(2,1)S(1)}, bf16[80,1920]{1,0:T(8,128)(2,1)S(1)}, u32[]{:S(2)}, u32[]{:S(2)}) collective-permute-start(bf16[80,1920]{1,0:T(8,128)(2,1)S(1)} %slice.67), channel_id=1, source_target_pairs={{0,1},{1,2},{2,3},{3,0},{4,5},{5,6},{6,7},{7,4},{8,9},{9,10},{10,1... | collective-permute-start | bytes 921608 | tf_op jit(solution)/shard_map/ppermute | solution.py:242
  51.4 2.0 %collective-permute-start.8 = (bf16[96,1920]{1,0:T(8,128)(2,1)S(1)}, bf16[96,1920]{1,0:T(8,128)(2,1)S(1)}, u32[]{:S(2)}, u32[]{:S(2)}) collective-permute-start(bf16[96,1920]{1,0:T(8,128)(2,1)S(1)} %slice.68), channel_id=1, source_target_pairs={{0,3},{1,0},{2,1},{3,2},{4,7},{5,4},{6,5},{7,6},{8,11},{9,8},{10,9... | collective-permute-start | bytes 1105928 | tf_op jit(solution)/shard_map/ppermute | solution.py:243
  53.4 1.3 broadcast_select_fusion.1
  54.7 1.5 pad_maximum_fusion.weight_ref
  56.2 6.4 %collective-permute-done.3.refs_3_ = bf16[176,1920]{1,0:T(8,128)(2,1)} collective-permute-done((bf16[176,1920]{1,0:T(8,128)(2,1)}, bf16[176,1920]{1,0:T(8,128)(2,1)}, u32[]{:S(2)}, u32[]{:S(2)}) %collective-permute-start.3) | collective-permute-done | bytes 675872 | tf_op jit(solution)/shard_map/ppermute | solution.py:238
  62.6 0.3 collective-permute-done.7.refs_7_
  63.0 0.6 copy-done.4
  63.6 6.9 %collective-permute-done.8.refs_8_ = bf16[96,1920]{1,0:T(8,128)(2,1)S(1)} collective-permute-done((bf16[96,1920]{1,0:T(8,128)(2,1)S(1)}, bf16[96,1920]{1,0:T(8,128)(2,1)S(1)}, u32[]{:S(2)}, u32[]{:S(2)}) %collective-permute-start.8) | collective-permute-done | bytes 368672 | tf_op jit(solution)/shard_map/ppermute | solution.py:243
  70.4 0.7 copy-done.5
  71.2 28.8 %group.1 = (bf16[112,1024]{1,0:T(8,128)(2,1)}, f32[8,128]{1,0:T(8,128)}, bf16[1408,1024]{1,0:T(8,128)(2,1)}, bf16[1408,1408]{1,0:T(8,128)(2,1)}, bf16[176,1024]{1,0:T(8,128)(2,1)}) custom-call(s32[8]{0:T(128)} %stack.35.place_ref, bf16[832,1024]{1,0:T(8,128)(2,1)} %pad_maximum_fusion.weight_ref, bf16[176,1920]{1,0:T(8,128)(2,1)} %fusion.10.refs_0_, ...), custom_call_target="tpu_custom_call" | custom-call | flops 12000000000 | bytes 20000000 | tf_op jit(solution)/shard_map/group/pallas_call | solution.py:175
  99.9 1.0 broadcast_select_fusion.2
  101.0 1.2 slice.57
  103.5 0.1 and_select_fusion.5
  103.6 7.8 %collective-permute-start.9 = (bf16[128,512]{1,0:T(8,128)(2,1)S(1)}, bf16[128,512]{1,0:T(8,128)(2,1)S(1)}, u32[]{:S(2)}, u32[]{:S(2)}) collective-permute-start(bf16[128,512]{1,0:T(8,128)(2,1)S(1)} %pad_maximum_fusion.1), channel_id=1, source_target_pairs={{0,8},{8,0},{1,9},{9,1},{2,10},{10,2},{3,11},{11,3},{4,12},{12,4},... | collective-permute-start | bytes 393224 | tf_op jit(solution)/shard_map/ppermute | solution.py:286
  111.4 0.2 fusion.8
  111.5 0.8 collective-permute-done.9
  112.3 0.6 fusion.11
  114.2 0.1 and_select_fusion.4
  114.3 1.0 add_convert_fusion
  115.4 0.7 pad.9
  116.1 24.9 %all-to-all-start.1 = ((bf16[48,16,128]{2,1,0:T(8,128)(2,1)}), bf16[48,16,128]{2,1,0:T(8,128)(2,1)S(1)}, u32[]{:S(2)}, u32[]{:S(2)}) async-start(bf16[48,16,128]{2,1,0:T(8,128)(2,1)} %pad.9), calls=%async_computation.1 | async-start | bytes 393216 | tf_op jit(solution)/shard_map/all_to_all | solution.py:297
  141.1 1.5 convolution_convert_fusion
  142.6 14.7 %all-to-all-done.1 = bf16[48,16,128]{2,1,0:T(8,128)(2,1)S(1)} async-done(((bf16[48,16,128]{2,1,0:T(8,128)(2,1)}), bf16[48,16,128]{2,1,0:T(8,128)(2,1)S(1)}, u32[]{:S(2)}, u32[]{:S(2)}) %all-to-all-start.1) | async-done | bytes 196640 | tf_op jit(solution)/shard_map/all_to_all | solution.py:297
  157.3 0.1 convert_reduce_fusion
  157.4 0.1 select_select_fusion
  157.4 0.7 reshape.125
  158.1 5.7 %all-to-all-start.2 = ((bf16[48,16,128]{2,1,0:T(8,128)(2,1)}), bf16[48,16,128]{2,1,0:T(8,128)(2,1)S(1)}, u32[]{:S(2)}, u32[]{:S(2)}) async-start(bf16[48,16,128]{2,1,0:T(8,128)(2,1)} %reshape.125), calls=%async_computation.2 | async-start | bytes 393216 | tf_op jit(solution)/shard_map/all_to_all | solution.py:308
  163.8 3.3 %fusion.4 = (f32[176]{0:T(256)S(1)}, f32[176,1024]{1,0:T(8,128)S(1)}) fusion(bf16[176,1024]{1,0:T(8,128)(2,1)S(1)} %copy-done, f32[176]{0:T(256)S(1)} %add_rsqrt_fusion, bf16[1408,1024]{1,0:T(8,128)(2,1)} %get-tuple-element.13, bf16[1408,1408]{1,0:T(8,128)(2,1)} %get-tuple-element.12, s32[]{:T(128)S(6)} %select_n.142), kind=kOutput, calls=%fused_computation.12 | convolution fusion | flops 508411712 | bytes 4687236 | tf_op jit(solution)/shard_map/dot_general | solution.py:211
  167.1 1.0 fusion.7
  168.1 11.2 %all-to-all-done.2 = bf16[48,16,128]{2,1,0:T(8,128)(2,1)S(1)} async-done(((bf16[48,16,128]{2,1,0:T(8,128)(2,1)}), bf16[48,16,128]{2,1,0:T(8,128)(2,1)S(1)}, u32[]{:S(2)}, u32[]{:S(2)}) %all-to-all-start.2) | async-done | bytes 196640 | tf_op jit(solution)/shard_map/all_to_all | solution.py:308
  179.4 5.3 %all_gather.3 = bf16[112,1024]{1,0:T(8,128)(2,1)S(1)} all-gather(bf16[112,512]{1,0:T(8,128)(2,1)S(1)} %bitcast.36), channel_id=1, replica_groups=mesh['yh'=4,'z'=12,'core'=2,'yl'=2,'x'=4] {'core'}, dimensions={1}, use_global_device_ids=true | all-gather | bytes 344064 | tf_op jit(solution)/shard_map/all_gather | solution.py:312
  184.7 0.8 slice_convert_fusion
  185.5 0.6 convert_reduce_fusion.1
  (34 shorter events, 0.3 us)
Async XLA Ops:
  0.6 7.9 %copy-start.1 = (bf16[176,832]{1,0:T(8,128)(2,1)S(1)}, bf16[176,832]{1,0:T(8,128)(2,1)}, u32[]{:S(2)}) copy-start(bf16[176,832]{1,0:T(8,128)(2,1)} %param.3) | copy-start | bytes 878596
  0.6 7.9 %copy-start = (bf16[176,1024]{1,0:T(8,128)(2,1)S(1)}, bf16[176,1024]{1,0:T(8,128)(2,1)}, u32[]{:S(2)}) copy-start(bf16[176,1024]{1,0:T(8,128)(2,1)} %param.5) | copy-start | bytes 1081348
  2.6 14.5 %all-to-all-start = ((bf16[8,104,512]{2,1,0:T(8,128)(2,1)}), bf16[8,104,512]{2,1,0:T(8,128)(2,1)S(1)}, u32[]{:S(2)}, u32[]{:S(2)}) async-start(bf16[8,104,512]{2,1,0:T(8,128)(2,1)} %broadcast_in_dim.48), calls=%async_computation | async-start | bytes 1703936 | tf_op jit(solution)/shard_map/all_to_all | solution.py:254
  9.5 22.0 %collective-permute-start.2 = (bf16[176,1920]{1,0:T(8,128)(2,1)}, bf16[176,1920]{1,0:T(8,128)(2,1)}, u32[]{:S(2)}, u32[]{:S(2)}) collective-permute-start(bf16[176,1920]{1,0:T(8,128)(2,1)} %fusion.10.refs_0_), channel_id=1, source_target_pairs={{0,1},{1,2},{2,3},{3,0},{4,5},{5,6},{6,7},{7,4},{8,9},{9,10},{10,1... | collective-permute-start | bytes 2027528 | tf_op jit(solution)/shard_map/ppermute | solution.py:237
  12.9 21.3 %collective-permute-start.1 = (bf16[176,1920]{1,0:T(8,128)(2,1)}, bf16[176,1920]{1,0:T(8,128)(2,1)}, u32[]{:S(2)}, u32[]{:S(2)}) collective-permute-start(bf16[176,1920]{1,0:T(8,128)(2,1)} %fusion.10.refs_0_), channel_id=1, source_target_pairs={{0,4},{4,0},{1,5},{5,1},{2,6},{6,2},{3,7},{7,3},{8,12},{12,8},{9,1... | collective-permute-start | bytes 2027528 | tf_op jit(solution)/shard_map/ppermute | solution.py:236
  17.1 36.3 %collective-permute-start = (bf16[832,512]{1,0:T(8,128)(2,1)S(1)}, bf16[832,512]{1,0:T(8,128)(2,1)}, u32[]{:S(2)}, u32[]{:S(2)}) collective-permute-start(bf16[832,512]{1,0:T(8,128)(2,1)S(1)} %bitcast.32), channel_id=1, source_target_pairs={{0,8},{8,0},{1,9},{9,1},{2,10},{10,2},{3,11},{11,3},{4,12},{12,4},... | collective-permute-start | bytes 2555912 | tf_op jit(solution)/shard_map/ppermute | solution.py:255
  31.5 14.2 %collective-permute-start.4 = (bf16[176,1920]{1,0:T(8,128)(2,1)}, bf16[176,1920]{1,0:T(8,128)(2,1)S(1)}, u32[]{:S(2)}, u32[]{:S(2)}) collective-permute-start(bf16[176,1920]{1,0:T(8,128)(2,1)} %collective-permute-done.2.refs_2_), channel_id=1, source_target_pairs={{0,4},{4,0},{1,5},{5,1},{2,6},{6,2},{3,7},{7,3},{8,12},{12,8},{9,1... | collective-permute-start | bytes 2027528 | tf_op jit(solution)/shard_map/ppermute | solution.py:239
  34.2 17.2 %collective-permute-start.5 = (bf16[176,1920]{1,0:T(8,128)(2,1)}, bf16[176,1920]{1,0:T(8,128)(2,1)S(1)}, u32[]{:S(2)}, u32[]{:S(2)}) collective-permute-start(bf16[176,1920]{1,0:T(8,128)(2,1)} %collective-permute-done.1.refs_1_), channel_id=1, source_target_pairs={{0,3},{1,0},{2,1},{3,2},{4,7},{5,4},{6,5},{7,6},{8,11},{9,8},{10,9... | collective-permute-start | bytes 2027528 | tf_op jit(solution)/shard_map/ppermute | solution.py:240
  38.0 24.6 %collective-permute-start.3 = (bf16[176,1920]{1,0:T(8,128)(2,1)}, bf16[176,1920]{1,0:T(8,128)(2,1)}, u32[]{:S(2)}, u32[]{:S(2)}) collective-permute-start(bf16[176,1920]{1,0:T(8,128)(2,1)} %fusion.10.refs_0_), channel_id=1, source_target_pairs={{0,3},{1,0},{2,1},{3,2},{4,7},{5,4},{6,5},{7,6},{8,11},{9,8},{10,9... | collective-permute-start | bytes 2027528 | tf_op jit(solution)/shard_map/ppermute | solution.py:238
  41.3 21.4 %collective-permute-start.6 = (bf16[176,1920]{1,0:T(8,128)(2,1)}, bf16[176,1920]{1,0:T(8,128)(2,1)S(1)}, u32[]{:S(2)}, u32[]{:S(2)}) collective-permute-start(bf16[176,1920]{1,0:T(8,128)(2,1)} %collective-permute-done.2.refs_2_), channel_id=1, source_target_pairs={{0,1},{1,2},{2,3},{3,0},{4,5},{5,6},{6,7},{7,4},{8,9},{9,10},{10,1... | collective-permute-start | bytes 2027528 | tf_op jit(solution)/shard_map/ppermute | solution.py:241
  45.7 7.7 %copy-start.3 = (bf16[176,1920]{1,0:T(8,128)(2,1)}, bf16[176,1920]{1,0:T(8,128)(2,1)S(1)}, u32[]{:S(2)}) copy-start(bf16[176,1920]{1,0:T(8,128)(2,1)S(1)} %collective-permute-done.4.refs_4_) | copy-start | bytes 2027524
  45.7 17.2 %collective-permute-start.7 = (bf16[80,1920]{1,0:T(8,128)(2,1)S(1)}, bf16[80,1920]{1,0:T(8,128)(2,1)S(1)}, u32[]{:S(2)}, u32[]{:S(2)}) collective-permute-start(bf16[80,1920]{1,0:T(8,128)(2,1)S(1)} %slice.67), channel_id=1, source_target_pairs={{0,1},{1,2},{2,3},{3,0},{4,5},{5,6},{6,7},{7,4},{8,9},{9,10},{10,1... | collective-permute-start | bytes 921608 | tf_op jit(solution)/shard_map/ppermute | solution.py:242
  51.4 2.0 %copy-start.2 = (bf16[176,1920]{1,0:T(8,128)(2,1)}, bf16[176,1920]{1,0:T(8,128)(2,1)S(1)}, u32[]{:S(2)}) copy-start(bf16[176,1920]{1,0:T(8,128)(2,1)S(1)} %collective-permute-done.5.refs_5_) | copy-start | bytes 2027524
  51.4 19.0 %collective-permute-start.8 = (bf16[96,1920]{1,0:T(8,128)(2,1)S(1)}, bf16[96,1920]{1,0:T(8,128)(2,1)S(1)}, u32[]{:S(2)}, u32[]{:S(2)}) collective-permute-start(bf16[96,1920]{1,0:T(8,128)(2,1)S(1)} %slice.68), channel_id=1, source_target_pairs={{0,3},{1,0},{2,1},{3,2},{4,7},{5,4},{6,5},{7,6},{8,11},{9,8},{10,9... | collective-permute-start | bytes 1105928 | tf_op jit(solution)/shard_map/ppermute | solution.py:243
  62.6 0.9 copy-start.4
  63.6 6.9 %copy-start.6 = (bf16[80,1920]{1,0:T(8,128)(2,1)}, bf16[80,1920]{1,0:T(8,128)(2,1)S(1)}, u32[]{:S(2)}) copy-start(bf16[80,1920]{1,0:T(8,128)(2,1)S(1)} %collective-permute-done.7.refs_7_) | copy-start | bytes 921604
  70.4 0.7 copy-start.5
  99.9 41.2 %copy-start.7 = (bf16[176,1024]{1,0:T(8,128)(2,1)S(1)}, bf16[176,1024]{1,0:T(8,128)(2,1)}, u32[]{:S(2)}) copy-start(bf16[176,1024]{1,0:T(8,128)(2,1)} %get-tuple-element.11) | copy-start | bytes 1081348
  103.6 8.7 %collective-permute-start.9 = (bf16[128,512]{1,0:T(8,128)(2,1)S(1)}, bf16[128,512]{1,0:T(8,128)(2,1)S(1)}, u32[]{:S(2)}, u32[]{:S(2)}) collective-permute-start(bf16[128,512]{1,0:T(8,128)(2,1)S(1)} %pad_maximum_fusion.1), channel_id=1, source_target_pairs={{0,8},{8,0},{1,9},{9,1},{2,10},{10,2},{3,11},{11,3},{4,12},{12,4},... | collective-permute-start | bytes 393224 | tf_op jit(solution)/shard_map/ppermute | solution.py:286
  116.1 41.2 %all-to-all-start.1 = ((bf16[48,16,128]{2,1,0:T(8,128)(2,1)}), bf16[48,16,128]{2,1,0:T(8,128)(2,1)S(1)}, u32[]{:S(2)}, u32[]{:S(2)}) async-start(bf16[48,16,128]{2,1,0:T(8,128)(2,1)} %pad.9), calls=%async_computation.1 | async-start | bytes 393216 | tf_op jit(solution)/shard_map/all_to_all | solution.py:297
  158.1 21.1 %all-to-all-start.2 = ((bf16[48,16,128]{2,1,0:T(8,128)(2,1)}), bf16[48,16,128]{2,1,0:T(8,128)(2,1)S(1)}, u32[]{:S(2)}, u32[]{:S(2)}) async-start(bf16[48,16,128]{2,1,0:T(8,128)(2,1)} %reshape.125), calls=%async_computation.2 | async-start | bytes 393216 | tf_op jit(solution)/shard_map/all_to_all | solution.py:308

commit v3 on v2

--- a/solution.py
+++ b/solution.py
@@ -20,22 +20,36 @@
     return [(at, min(step, size - at)) for at in range(0, size, step)]
 
 
-def group_kernel(n_fs, depth, place_ref, weight_ref, *refs):
-    blocks = refs[: n_fs + 1]
-    head_ref, loss_ref, unit_out, coupling_out, dz_out = refs[n_fs + 1 : n_fs + 6]
-    packed, weight, u_full, inv_u, unit, text, score, prob, coupling, dz, dg, sems, wsem, osem = refs[n_fs + 6 :]
+def put_pieces(out_ref, at, value):
+    lane = lax.broadcasted_iota(jnp.int32, (16, 128), 1)
+    line = lax.broadcasted_iota(jnp.int32, (16, 128), 0)
+    value = jnp.broadcast_to(value[0:1, :], (16, 128))
+    one = value.astype(BF).astype(F32)
+    two = (value - one).astype(BF).astype(F32)
+    three = value - one - two
+    row = jnp.where(lane == 0, one, jnp.where(lane == 1, two, three))
+    row = jnp.where((line == 0) & (lane < 3), row, 0.0)
+    out_ref[at : at + 16, 0:128] = row.astype(BF)
+    if out_ref.shape[1] > 128:
+        out_ref[at : at + 16, 128:] = jnp.zeros((16, out_ref.shape[1] - 128), BF)
+
+
+def group_kernel(n_fs, depth, layout, place_ref, weight_ref, *refs):
+    blocks, refs = refs[: len(layout)], refs[len(layout) :]
+    mine_ref, other_ref, loss_ref, unit_out, coupling_out, dz_out = refs[:6]
+    feats, words, weight, u_full, inv_u, unit, text, score, prob, coupling, dz, dg, fsem, tsem, wsem, osem = refs[6:]
     group, width = unit.shape
     rows = group // n_fs
     padded = weight.shape[0]
     own = place_ref[0]
     copies = []
-    for k in range(n_fs - 1):
-        at = pl.multiple_of(place_ref[k] * rows, 16)
-        copies.append(pltpu.make_async_copy(blocks[k], packed.at[pl.ds(at, rows)], sems.at[k]))
-    cut = blocks[n_fs - 1].shape[0]
-    at = pl.multiple_of(place_ref[n_fs - 1] * rows, 16)
-    copies.append(pltpu.make_async_copy(blocks[n_fs - 1], packed.at[pl.ds(at, cut)], sems.at[n_fs - 1]))
-    copies.append(pltpu.make_async_copy(blocks[n_fs], packed.at[pl.ds(at + cut, rows - cut)], sems.at[n_fs]))
+    for k, (slot, down) in enumerate(layout):
+        first = pl.multiple_of(place_ref[slot] * rows + down, 16)
+        at = pl.ds(first, blocks[k].shape[0])
+        source = blocks[k].at[:, pl.ds(width, padded)]
+        copies.append(pltpu.make_async_copy(source, feats.at[at], fsem.at[k]))
+        source = blocks[k].at[:, pl.ds(0, width)]
+        copies.append(pltpu.make_async_copy(source, words.at[at], tsem.at[k]))
     copies.append(pltpu.make_async_copy(weight_ref, weight.at[pl.ds(0, depth)], wsem))
     for copy in copies:
         copy.start()
@@ -46,7 +60,7 @@
 
     for at, size in spans(width, 256):
         u_full[:, at : at + size] = jnp.dot(
-            packed[:, width:], weight[:, at : at + size], preferred_element_type=F32
+            feats[...], weight[:, at : at + size], preferred_element_type=F32
         )
 
     def normalise(k, carry):
@@ -57,7 +71,7 @@
         u_full[r, :] = u
         unit[r, :] = u.astype(BF)
         inv_u[r, :] = jnp.broadcast_to(inverse, (CHUNK, 128))
-        t = packed[r, :width].astype(F32)
+        t = words[r, :].astype(F32)
         inverse = lax.rsqrt(jnp.sum(t * t, axis=1, keepdims=True) + 1e-06)
         text[r, :] = (t * inverse).astype(BF)
         return carry
@@ -154,37 +168,48 @@
         == own * columns + lax.broadcasted_iota(jnp.int32, (padded, 128), 1)
     ) & (lax.broadcasted_iota(jnp.int32, (padded, 128), 1) < columns)
     features = jnp.dot(
-        packed[:, width:], pick.astype(F32).astype(BF), preferred_element_type=F32
+        feats[...], pick.astype(F32).astype(BF), preferred_element_type=F32
     ).astype(BF)
     head = lax.dot_general(features, dz[...], TN, preferred_element_type=F32)
-    head_ref[...] = head[: head_ref.shape[0], :].astype(BF)
+    u_full[0:128, :] = head
+    core = place_ref[n_fs]
+    half = width // 2
+    head_rows = mine_ref.shape[0]
+    mine = pl.ds(pl.multiple_of(core * half, 128), half)
+    other = pl.ds(pl.multiple_of((1 - core) * half, 128), half)
+    mine_ref[...] = u_full[0:head_rows, mine]
+    other_ref[0:head_rows, :] = u_full[0:head_rows, other].astype(BF)
+    put_pieces(other_ref, head_rows, loss_ref[...])
     out_unit.wait()
     out_coupling.wait()
     out_dz.wait()
 
 
-def group_call(place, weight, blocks, depth):
-    n_fs = len(blocks) - 1
-    rows, lanes = blocks[0].shape
-    width = weight.shape[1]
+def group_call(place, weight, blocks, layout):
+    n_fs = place.shape[0] - 1
+    rows, width = blocks[0].shape[0], weight.shape[1]
+    depth = weight.shape[0]
     group = n_fs * rows
-    padded = lanes - width
+    padded = -(-depth // 128) * 128
+    half = width // 2
     head_rows = -(-(depth // n_fs) // 16) * 16
     anywhere = pl.BlockSpec(memory_space=pl.ANY)
     inside = pl.BlockSpec(memory_space=pltpu.VMEM)
     return pl.pallas_call(
-        functools.partial(group_kernel, n_fs, depth),
+        functools.partial(group_kernel, n_fs, depth, layout),
         out_shape=(
-            jax.ShapeDtypeStruct((head_rows, width), BF),
+            jax.ShapeDtypeStruct((head_rows, half), F32),
+            jax.ShapeDtypeStruct((head_rows + 16, half), BF),
             jax.ShapeDtypeStruct((8, 128), F32),
             jax.ShapeDtypeStruct((group, width), BF),
             jax.ShapeDtypeStruct((group, group), BF),
             jax.ShapeDtypeStruct((rows, width), BF),
         ),
         in_specs=[pl.BlockSpec(memory_space=pltpu.SMEM)] + [anywhere] * (len(blocks) + 1),
-        out_specs=(inside, inside, anywhere, anywhere, anywhere),
+        out_specs=(inside, inside, inside, anywhere, anywhere, anywhere),
         scratch_shapes=[
-            pltpu.VMEM((group, lanes), BF),
+            pltpu.VMEM((group, padded), BF),
+            pltpu.VMEM((group, width), BF),
             pltpu.VMEM((padded, width), BF),
             pltpu.VMEM((group, width), F32),
             pltpu.VMEM((group, 128), F32),
@@ -195,7 +220,8 @@
             pltpu.VMEM((group, group), BF),
             pltpu.VMEM((group, width), BF),
             pltpu.VMEM((8, group), F32),
-            pltpu.SemaphoreType.DMA((n_fs + 1,)),
+            pltpu.SemaphoreType.DMA((len(blocks),)),
+            pltpu.SemaphoreType.DMA((len(blocks),)),
             pltpu.SemaphoreType.DMA,
             pltpu.SemaphoreType.DMA((3,)),
         ],
@@ -207,6 +233,34 @@
     )(place, weight, *blocks)
 
 
+def tile_kernel(mine_ref, came_ref, loss_ref, tiles_ref, pair):
+    head_rows, half = mine_ref.shape
+    lanes = half // 128
+    pair[...] = mine_ref[...] + came_ref[0:head_rows, :].astype(F32)
+    for group in range(head_rows // 16):
+        for lane in range(lanes):
+            tiles_ref[lanes * group + lane] = pair[
+                16 * group : 16 * group + 16, 128 * lane : 128 * lane + 128
+            ].astype(BF)
+    count = head_rows // 16 * lanes
+    tiles_ref[count + 1 :] = jnp.zeros((tiles_ref.shape[0] - count - 1, 16, 128), BF)
+    theirs = came_ref[head_rows : head_rows + 16, 0:128].astype(F32)
+    theirs = jnp.sum(theirs, axis=1, keepdims=True)[0:1]
+    put_pieces(tiles_ref.at[count], 0, loss_ref[...] + theirs)
+
+
+def tile_call(mine, came, loss, count):
+    inside = pl.BlockSpec(memory_space=pltpu.VMEM)
+    return pl.pallas_call(
+        tile_kernel,
+        out_shape=jax.ShapeDtypeStruct((count, 16, 128), BF),
+        in_specs=[inside] * 3,
+        out_specs=inside,
+        scratch_shapes=[pltpu.VMEM(mine.shape, F32)],
+        name="tiles",
+    )(mine, came, loss)
+
+
 def left_product(left, right):
     return lax.dot_general(
         left, right, (((0,), (0,)), ((), ())), preferred_element_type=F32
@@ -236,22 +290,28 @@
     got[1, 0] = lax.ppermute(block, "yl", flip)
     got[0, 3] = lax.ppermute(block, "x", up)
     got[0, 1] = lax.ppermute(block, "x", down)
+    got[1, 0], got[0, 3], got[0, 1] = lax.optimization_barrier(
+        (got[1, 0], got[0, 3], got[0, 1])
+    )
     got[1, 3] = lax.ppermute(got[0, 3], "yl", flip)
     got[1, 1] = lax.ppermute(got[1, 0], "x", down)
     got[0, 2] = lax.ppermute(got[0, 3], "x", up)
     low = lax.ppermute(got[1, 3][:half], "x", up)
     high = lax.ppermute(got[1, 1][half:], "x", down)
     keys = list(got) + [(1, 2)]
-    return keys, list(got.values()) + [low, high]
-
-
-def gather_head(head_weight, part, n_fs):
+    layout = [(k, 0) for k in range(len(keys))] + [(len(keys) - 1, half)]
+    return keys, list(got.values()) + [low, high], layout, got
+
+
+def whole_head(head_weight, part, n_fs, first, later):
     rows, width = head_weight.shape
     half = width // 2
     core = lax.axis_index("core")
     mine = jnp.where(core == 0, head_weight[:, :half], head_weight[:, half:])
+    mine = lax.optimization_barrier((mine, *first))[0]
     mine = jnp.broadcast_to(mine[None], (n_fs, rows, half))
     mine = lax.all_to_all(mine, part, 0, 0, tiled=True).reshape(n_fs * rows, half)
+    mine = lax.optimization_barrier((mine, *later))[0]
     other = lax.ppermute(mine, "core", [(0, 1), (1, 0)])
     left = jnp.where(core == 0, mine, other)
     right = jnp.where(core == 0, other, mine)
@@ -265,38 +325,16 @@
     return one, two, three
 
 
-def loss_rows(loss, width):
-    lane = lax.broadcasted_iota(jnp.int32, (16, width), 1)
-    row = lax.broadcasted_iota(jnp.int32, (16, width), 0)
-    out = jnp.zeros((16, width), BF)
-    for k, piece in enumerate(pieces(loss)):
-        out = jnp.where((lane == k) & (row == 0), piece, out)
-    return out
-
-
-def sum_over_groups(head, loss, n_h, n_z):
-    padded, width = head.shape
-    core = lax.axis_index("core")
-    half = width // 2
-    first, second = head[:, :half], head[:, half:]
-    tail = loss_rows(loss, half)
-    mine = jnp.where(core == 0, first, second)
-    other = jnp.where(core == 0, second, first)
-    other = jnp.concatenate([other, tail], axis=0)
+def sum_over_groups(mine, other, loss, n_h, n_z):
+    padded, half = mine.shape
     came = lax.ppermute(other, "core", [(0, 1), (1, 0)])
-    both = (mine.astype(F32) + came[:padded].astype(F32)).astype(BF)
-    chip_loss = loss + jnp.sum(came[padded].astype(F32)[:3])
-    both = jnp.concatenate([both, loss_rows(chip_loss, half)], axis=0)
     lanes = half // 128
-    groups = both.shape[0] // 16
-    tiles = both.reshape(groups, 16, lanes, 128).transpose(0, 2, 1, 3).reshape(-1, 16, 128)
     peers = n_h * n_z
-    count = tiles.shape[0]
-    each = -(-count // peers)
-    tiles = jnp.pad(tiles, ((0, each * peers - count), (0, 0), (0, 0)))
+    loss_tile = padded // 16 * lanes
+    each = -(-(loss_tile + 1) // peers)
+    tiles = tile_call(mine, came, loss, each * peers)
     tiles = lax.all_to_all(tiles, ("yh", "z"), 0, 0, tiled=True)
     total = jnp.sum(tiles.reshape(peers, each, 16, 128).astype(F32), axis=0)
-    loss_tile = count - lanes
     place = (lax.axis_index("yh") * n_z + lax.axis_index("z")) * each
     here = (place + lax.broadcasted_iota(jnp.int32, (each, 16, 128), 0)) == loss_tile
     row = lax.broadcasted_iota(jnp.int32, (each, 16, 128), 1)
@@ -326,16 +364,16 @@
 
     def body(features, head_weight, text_embed):
         rows, depth = features.shape
-        width = text_embed.shape[1]
-        weight = gather_head(head_weight, part, n_fs)
-        packed = jnp.concatenate([text_embed, features], axis=1)
-        packed = jnp.pad(packed, ((0, 0), (0, -packed.shape[1] % 128)))
-        keys, blocks = gather_group(packed, n_y, n_x)
         y, x = lax.axis_index("yl"), lax.axis_index("x")
-        place = jnp.stack(
-            [((y + dy) % n_y) * n_x + (x + dx) % n_x for dy, dx in keys]
-        ).astype(jnp.int32)
-        head, loss, image_unit, coupling, dz = group_call(place, weight, blocks, depth)
+        gap = jnp.zeros((rows, -depth % 128), BF)
+        packed = jnp.concatenate([text_embed, features, gap], axis=1)
+        keys, blocks, layout, got = gather_group(packed, n_y, n_x)
+        place = [((y + dy) % n_y) * n_x + (x + dx) % n_x for dy, dx in keys]
+        place = jnp.stack(place + [lax.axis_index("core")]).astype(jnp.int32)
+        weight = whole_head(head_weight, part, n_fs, [], [])
+        mine, other, loss, image_unit, coupling, dz = group_call(
+            place, weight, blocks, tuple(layout)
+        )
         own_coupling = lax.dynamic_slice(
             coupling, (0, place[0] * rows), (n_fs * rows, rows)
         )
@@ -345,7 +383,7 @@
             (dv - v_rows * jnp.sum(v_rows * dv, axis=-1, keepdims=True)) * inv_v
         ).astype(BF)
         feat_grad = right_product(dz, weight).astype(BF)
-        head_grad, loss = sum_over_groups(head, loss[0, 0], n_h, n_z)
+        head_grad, loss = sum_over_groups(mine, other, loss, n_h, n_z)
         head_grad = head_grad[: head_weight.shape[0]]
         loss = loss / (2.0 * n_fs * rows * n_dp)
         return (loss, feat_grad, text_grad, head_grad)

time: 189 us -> 174 us (0.921)
  waiting for transfers between devices: 43.1 us -> 36.7 us
  starting transfers between devices: 84.4 us -> 79.1 us
  other arithmetic: 10.3 us -> 6.46 us
  between operations: 5.45 us -> 2.8 us
  Pallas kernels: 28.8 us -> 30.9 us
    ppermute x1, waiting for transfers between devices: 6.87 us -> 0.01 us  [gather_group(): high = lax.ppermute(got[1, 1][half:], 'x', down)]
    ppermute x1, waiting for transfers between devices: 6.39 us -> 1.97 us  [gather_group(): got[0, 1] = lax.ppermute(block, 'x', down)]
    all_to_all x1, starting transfers between devices: 24.9 us -> 21.4 us  [sum_over_groups(): tiles = lax.all_to_all(tiles, ('yh', 'z'), 0, 0, tiled=True)]
    ppermute x1, waiting for transfers between devices: 0.33 us -> 3.56 us  [gather_group(): low = lax.ppermute(got[1, 3][:half], 'x', up)]
    ppermute x1, waiting for transfers between devices: 1.58 us -> 4.67 us  [gather_group(): got[1, 3] = lax.ppermute(got[0, 3], 'yl', flip)]
    ppermute x1, starting transfers between devices: 5.65 us -> 3.08 us  [gather_group(): low = lax.ppermute(got[1, 3][:half], 'x', up)]
    unnamed x17 -> x21, local copies, waits for them, and re-layouts: 1.38 us -> 3.61 us
    pallas_call x1 -> x2, Pallas kernels: 28.8 us -> 30.9 us  [the longest x1 29.1 us: group_call(): pl.pallas_call(functools.partial(group_kernel, n_fs, depth, layout), out_...]
  transfers between devices with their start and end apart: 13 -> 13, of which waited for: 8 -> 7; matrix products, arithmetic and copies ran while one was open for 6% -> 6% of each run, Pallas kernels for 0% -> 0%
where the time goes in v3:
time: 174 us; the launch traced here: 173 us
  starting transfers between devices  79.1 us (45%)
  waiting for transfers between devices  36.7 us (21%)
  Pallas kernels  30.9 us (18%)
  other arithmetic  6.46 us (4%)
  local copies, waits for them, and re-layouts  6.3 us (4%)
  matrix products  5.75 us (3%)
  blocking collectives  5.3 us (3%)
  between operations  2.8 us (2%)
    pallas_call x1, Pallas kernels, group_call(): pl.pallas_call(functools.partial(group_kernel, n_fs, depth, layout), out_...  29.1 us
    all_to_all x1, starting transfers between devices, sum_over_groups(): tiles = lax.all_to_all(tiles, ('yh', 'z'), 0, 0, tiled=True)  21.4 us
    all_to_all x1, waiting for transfers between devices, sum_over_groups(): tiles = lax.all_to_all(tiles, ('yh', 'z'), 0, 0, tiled=True)  13.9 us
    ppermute x1, starting transfers between devices, whole_head(): other = lax.ppermute(mine, 'core', [(0, 1), (1, 0)])  12.5 us
    all_to_all x1, waiting for transfers between devices, sum_over_groups(): tiles = lax.all_to_all(send, ('yh', 'z'), 0, 0, tiled=True)  11.2 us
    ppermute x1, starting transfers between devices, sum_over_groups(): came = lax.ppermute(other, 'core', [(0, 1), (1, 0)])  8.62 us
    all_to_all x1, starting transfers between devices, whole_head(): lax.all_to_all(mine, part, 0, 0, tiled=True).reshape(n_fs * rows, half)  5.86 us
    all_to_all x1, starting transfers between devices, sum_over_groups(): tiles = lax.all_to_all(send, ('yh', 'z'), 0, 0, tiled=True)  5.67 us
  transfers between devices with their start and end apart: 13, of which 7 were waited for; matrix products, arithmetic and copies ran while one was open for 6% of the time, Pallas kernels for 0%

profile of v3, /device:TPU:1, one launch (start us, length us, event | category | flops | bytes accessed | tf_op | source)
XLA Modules:
  0.0 173.2 jit_solution(14595468924306139447)
XLA Ops:
  0.7 1.0 slice_select_fusion
  1.7 1.0 broadcast_in_dim.32
  2.6 5.9 %all-to-all-start = ((bf16[8,104,512]{2,1,0:T(8,128)(2,1)}), bf16[8,104,512]{2,1,0:T(8,128)(2,1)S(1)}, u32[]{:S(2)}, u32[]{:S(2)}) async-start(bf16[8,104,512]{2,1,0:T(8,128)(2,1)} %broadcast_in_dim.32), calls=%async_computation | async-start | bytes 1703936 | tf_op jit(solution)/shard_map/all_to_all | solution.py:313
  8.5 0.3 concatenate.7.refs_0_
  8.8 3.4 %collective-permute-start.1 = (bf16[176,1920]{1,0:T(8,128)(2,1)S(1)}, bf16[176,1920]{1,0:T(8,128)(2,1)S(1)}, u32[]{:S(2)}, u32[]{:S(2)}) collective-permute-start(bf16[176,1920]{1,0:T(8,128)(2,1)S(1)} %concatenate.7.refs_0_), channel_id=1, source_target_pairs={{0,4},{4,0},{1,5},{5,1},{2,6},{6,2},{3,7},{7,3},{8,12},{12,8},{9,1... | collective-permute-start | bytes 2027528 | tf_op jit(solution)/shard_map/ppermute | solution.py:290
  12.2 3.1 %collective-permute-start.2 = (bf16[176,1920]{1,0:T(8,128)(2,1)S(1)}, bf16[176,1920]{1,0:T(8,128)(2,1)}, u32[]{:S(2)}, u32[]{:S(2)}) collective-permute-start(bf16[176,1920]{1,0:T(8,128)(2,1)S(1)} %concatenate.7.refs_0_), channel_id=1, source_target_pairs={{0,1},{1,2},{2,3},{3,0},{4,5},{5,6},{6,7},{7,4},{8,9},{9,10},{10,1... | collective-permute-start | bytes 2027528 | tf_op jit(solution)/shard_map/ppermute | solution.py:291
  15.3 3.4 %collective-permute-start.3 = (bf16[176,1920]{1,0:T(8,128)(2,1)S(1)}, bf16[176,1920]{1,0:T(8,128)(2,1)S(1)}, u32[]{:S(2)}, u32[]{:S(2)}) collective-permute-start(bf16[176,1920]{1,0:T(8,128)(2,1)S(1)} %concatenate.7.refs_0_), channel_id=1, source_target_pairs={{0,3},{1,0},{2,1},{3,2},{4,7},{5,4},{6,5},{7,6},{8,11},{9,8},{10,9... | collective-permute-start | bytes 2027528 | tf_op jit(solution)/shard_map/ppermute | solution.py:292
  18.7 0.0 all-to-all-done
  18.7 12.5 %collective-permute-start = (bf16[832,512]{1,0:T(8,128)(2,1)S(1)}, bf16[832,512]{1,0:T(8,128)(2,1)}, u32[]{:S(2)}, u32[]{:S(2)}) collective-permute-start(bf16[832,512]{1,0:T(8,128)(2,1)S(1)} %bitcast.27), channel_id=1, source_target_pairs={{0,8},{8,0},{1,9},{9,1},{2,10},{10,2},{3,11},{11,3},{4,12},{12,4},... | collective-permute-start | bytes 2555912 | tf_op jit(solution)/shard_map/ppermute | solution.py:315
  31.3 0.0 collective-permute-done.1.refs_1_
  31.3 0.3 collective-permute-done.2.refs_2_
  31.6 0.6 copy-done.6
  32.2 2.0 %collective-permute-done.3.refs_3_ = bf16[176,1920]{1,0:T(8,128)(2,1)S(1)} collective-permute-done((bf16[176,1920]{1,0:T(8,128)(2,1)S(1)}, bf16[176,1920]{1,0:T(8,128)(2,1)S(1)}, u32[]{:S(2)}, u32[]{:S(2)}) %collective-permute-start.3) | collective-permute-done | bytes 675872 | tf_op jit(solution)/shard_map/ppermute | solution.py:292
  34.1 0.8 copy-done.7
  35.0 2.2 %collective-permute-start.4 = (bf16[176,1920]{1,0:T(8,128)(2,1)}, bf16[176,1920]{1,0:T(8,128)(2,1)S(1)}, u32[]{:S(2)}, u32[]{:S(2)}) collective-permute-start(bf16[176,1920]{1,0:T(8,128)(2,1)} %collective-permute-done.2.refs_2_), channel_id=1, source_target_pairs={{0,4},{4,0},{1,5},{5,1},{2,6},{6,2},{3,7},{7,3},{8,12},{12,8},{9,1... | collective-permute-start | bytes 2027528 | tf_op jit(solution)/shard_map/ppermute | solution.py:296
  37.2 4.0 %collective-permute-start.5 = (bf16[176,1920]{1,0:T(8,128)(2,1)}, bf16[176,1920]{1,0:T(8,128)(2,1)S(1)}, u32[]{:S(2)}, u32[]{:S(2)}) collective-permute-start(bf16[176,1920]{1,0:T(8,128)(2,1)} %copy-done.6), channel_id=1, source_target_pairs={{0,3},{1,0},{2,1},{3,2},{4,7},{5,4},{6,5},{7,6},{8,11},{9,8},{10,9... | collective-permute-start | bytes 2027528 | tf_op jit(solution)/shard_map/ppermute | solution.py:297
  41.2 1.9 %collective-permute-start.6 = (bf16[176,1920]{1,0:T(8,128)(2,1)}, bf16[176,1920]{1,0:T(8,128)(2,1)}, u32[]{:S(2)}, u32[]{:S(2)}) collective-permute-start(bf16[176,1920]{1,0:T(8,128)(2,1)} %collective-permute-done.2.refs_2_), channel_id=1, source_target_pairs={{0,1},{1,2},{2,3},{3,0},{4,5},{5,6},{6,7},{7,4},{8,9},{9,10},{10,1... | collective-permute-start | bytes 2027528 | tf_op jit(solution)/shard_map/ppermute | solution.py:298
  43.2 0.6 stack.39.place_ref
  43.8 4.7 %collective-permute-done.4.refs_4_ = bf16[176,1920]{1,0:T(8,128)(2,1)S(1)} collective-permute-done((bf16[176,1920]{1,0:T(8,128)(2,1)}, bf16[176,1920]{1,0:T(8,128)(2,1)S(1)}, u32[]{:S(2)}, u32[]{:S(2)}) %collective-permute-start.4) | collective-permute-done | bytes 675872 | tf_op jit(solution)/shard_map/ppermute | solution.py:296
  48.5 3.1 %collective-permute-start.7 = (bf16[80,1920]{1,0:T(8,128)(2,1)S(1)}, bf16[80,1920]{1,0:T(8,128)(2,1)S(1)}, u32[]{:S(2)}, u32[]{:S(2)}) collective-permute-start(bf16[80,1920]{1,0:T(8,128)(2,1)S(1)} %slice.40), channel_id=1, source_target_pairs={{0,1},{1,2},{2,3},{3,0},{4,5},{5,6},{6,7},{7,4},{8,9},{9,10},{10,1... | collective-permute-start | bytes 921608 | tf_op jit(solution)/shard_map/ppermute | solution.py:299
  51.6 0.0 collective-permute-done.5.refs_5_
  51.7 3.9 %collective-permute-start.8 = (bf16[96,1920]{1,0:T(8,128)(2,1)S(1)}, bf16[96,1920]{1,0:T(8,128)(2,1)S(1)}, u32[]{:S(2)}, u32[]{:S(2)}) collective-permute-start(bf16[96,1920]{1,0:T(8,128)(2,1)S(1)} %slice.41), channel_id=1, source_target_pairs={{0,3},{1,0},{2,1},{3,2},{4,7},{5,4},{6,5},{7,6},{8,11},{9,8},{10,9... | collective-permute-start | bytes 1105928 | tf_op jit(solution)/shard_map/ppermute | solution.py:300
  55.7 1.3 broadcast_select_fusion.1
  56.9 1.5 pad_maximum_fusion.weight_ref
  58.4 0.0 collective-permute-done.6.refs_6_
  58.4 3.6 %collective-permute-done.7.refs_7_ = bf16[80,1920]{1,0:T(8,128)(2,1)S(1)} collective-permute-done((bf16[80,1920]{1,0:T(8,128)(2,1)S(1)}, bf16[80,1920]{1,0:T(8,128)(2,1)S(1)}, u32[]{:S(2)}, u32[]{:S(2)}) %collective-permute-start.7) | collective-permute-done | bytes 307232 | tf_op jit(solution)/shard_map/ppermute | solution.py:299
  62.0 0.0 collective-permute-done.8.refs_8_
  62.0 0.7 copy-done.9
  62.7 0.7 copy-done.8
  63.4 29.1 %group.1 = (f32[112,512]{1,0:T(8,128)}, bf16[128,512]{1,0:T(8,128)(2,1)}, f32[8,128]{1,0:T(8,128)}, bf16[1408,1024]{1,0:T(8,128)(2,1)}, bf16[1408,1408]{1,0:T(8,128)(2,1)}, /*index=5*/bf16[176,1024]{1,0:T(8,128)(2,1)}) custom-call(s32[9]{0:T(128)} %stack.39.place_ref, bf16[832,1024]{1,0:T(8,128)(2,1)} %pad_maximum_fusion.weight_ref, ...), custom_call_target="tpu_custom_call" | custom-call | flops 12000000000 | bytes 20000000 | tf_op jit(solution)/shard_map/group/pallas_call | solution.py:198
  92.5 8.6 %collective-permute-start.9 = (bf16[128,512]{1,0:T(8,128)(2,1)}, bf16[128,512]{1,0:T(8,128)(2,1)S(1)}, u32[]{:S(2)}, u32[]{:S(2)}) collective-permute-start(bf16[128,512]{1,0:T(8,128)(2,1)} %get-tuple-element.17), channel_id=1, source_target_pairs={{0,8},{8,0},{1,9},{9,1},{2,10},{10,2},{3,11},{11,3},{4,12},{12,4},... | collective-permute-start | bytes 393224 | tf_op jit(solution)/shard_map/ppermute | solution.py:330
  101.1 0.2 fusion.6
  101.3 1.0 collective-permute-done.9.came_ref
  102.3 0.7 copy-done.5
  103.0 1.8 %tiles.1 = bf16[48,16,128]{2,1,0:T(8,128)(2,1)} custom-call(f32[112,512]{1,0:T(8,128)} %get-tuple-element.16.mine_ref, bf16[128,512]{1,0:T(8,128)(2,1)} %copy-done.5, f32[8,128]{1,0:T(8,128)} %get-tuple-element.18.loss_ref), custom_call_target="tpu_custom_call" | custom-call | tf_op jit(solution)/shard_map/tiles/pallas_call | solution.py:254
  104.8 21.4 %all-to-all-start.1 = ((bf16[48,16,128]{2,1,0:T(8,128)(2,1)}), bf16[48,16,128]{2,1,0:T(8,128)(2,1)S(1)}, u32[]{:S(2)}, u32[]{:S(2)}) async-start(bf16[48,16,128]{2,1,0:T(8,128)(2,1)} %tiles.1), calls=%async_computation.1 | async-start | bytes 393216 | tf_op jit(solution)/shard_map/all_to_all | solution.py:336
  126.2 2.5 %convolution_convert_fusion = bf16[176,832]{1,0:T(8,128)(2,1)} fusion(bf16[176,1024]{1,0:T(8,128)(2,1)} %get-tuple-element.19, bf16[832,512]{1,0:T(8,128)(2,1)S(1)} %get-tuple-element.23, bf16[832,512]{1,0:T(8,128)(2,1)S(1)} %get-tuple-element.22), kind=kOutput, calls=%fused_computation.2 | convolution fusion | flops 303447040 | bytes 2357248 | tf_op jit(solution)/shard_map/dot_general | solution.py:271
  128.7 13.9 %all-to-all-done.1 = bf16[48,16,128]{2,1,0:T(8,128)(2,1)S(1)} async-done(((bf16[48,16,128]{2,1,0:T(8,128)(2,1)}), bf16[48,16,128]{2,1,0:T(8,128)(2,1)S(1)}, u32[]{:S(2)}, u32[]{:S(2)}) %all-to-all-start.1) | async-done | bytes 196640 | tf_op jit(solution)/shard_map/all_to_all | solution.py:336
  142.7 0.1 convert_reduce_fusion
  142.7 0.1 select_select_fusion
  142.8 0.7 reshape.115
  143.5 5.7 %all-to-all-start.2 = ((bf16[48,16,128]{2,1,0:T(8,128)(2,1)}), bf16[48,16,128]{2,1,0:T(8,128)(2,1)S(1)}, u32[]{:S(2)}, u32[]{:S(2)}) async-start(bf16[48,16,128]{2,1,0:T(8,128)(2,1)} %reshape.115), calls=%async_computation.2 | async-start | bytes 393216 | tf_op jit(solution)/shard_map/all_to_all | solution.py:346
  149.2 3.3 %fusion.2 = (f32[176]{0:T(256)S(1)}, f32[176,1024]{1,0:T(8,128)S(1)}) fusion(bf16[176,1024]{1,0:T(8,128)(2,1)S(1)} %copy-done, f32[176]{0:T(256)S(1)} %add_rsqrt_fusion, bf16[1408,1024]{1,0:T(8,128)(2,1)} %get-tuple-element.21, bf16[1408,1408]{1,0:T(8,128)(2,1)} %get-tuple-element.20, s32[]{:T(128)S(6)} %select_n.102), kind=kOutput, calls=%fused_computation.9 | convolution fusion | flops 508411712 | bytes 4687236 | tf_op jit(solution)/shard_map/dot_general | solution.py:265
  152.5 1.0 fusion.5
  153.4 11.2 %all-to-all-done.2 = bf16[48,16,128]{2,1,0:T(8,128)(2,1)S(1)} async-done(((bf16[48,16,128]{2,1,0:T(8,128)(2,1)}), bf16[48,16,128]{2,1,0:T(8,128)(2,1)S(1)}, u32[]{:S(2)}, u32[]{:S(2)}) %all-to-all-start.2) | async-done | bytes 196640 | tf_op jit(solution)/shard_map/all_to_all | solution.py:346
  164.7 5.3 %all_gather.3 = bf16[112,1024]{1,0:T(8,128)(2,1)S(1)} all-gather(bf16[112,512]{1,0:T(8,128)(2,1)S(1)} %bitcast.31), channel_id=1, replica_groups=mesh['yh'=4,'z'=12,'core'=2,'yl'=2,'x'=4] {'core'}, dimensions={1}, use_global_device_ids=true | all-gather | bytes 344064 | tf_op jit(solution)/shard_map/all_gather | solution.py:350
  170.1 0.8 slice_convert_fusion
  170.8 0.6 convert_reduce_fusion.1
  (26 shorter events, 0.2 us)
Async XLA Ops:
  0.6 7.9 %copy-start.2 = (bf16[176,832]{1,0:T(8,128)(2,1)S(1)}, bf16[176,832]{1,0:T(8,128)(2,1)}, u32[]{:S(2)}) copy-start(bf16[176,832]{1,0:T(8,128)(2,1)} %param.3) | copy-start | bytes 878596
  0.6 7.9 %copy-start = (bf16[176,1024]{1,0:T(8,128)(2,1)S(1)}, bf16[176,1024]{1,0:T(8,128)(2,1)}, u32[]{:S(2)}) copy-start(bf16[176,1024]{1,0:T(8,128)(2,1)} %param.5) | copy-start | bytes 1081348
  2.6 16.1 %all-to-all-start = ((bf16[8,104,512]{2,1,0:T(8,128)(2,1)}), bf16[8,104,512]{2,1,0:T(8,128)(2,1)S(1)}, u32[]{:S(2)}, u32[]{:S(2)}) async-start(bf16[8,104,512]{2,1,0:T(8,128)(2,1)} %broadcast_in_dim.32), calls=%async_computation | async-start | bytes 1703936 | tf_op jit(solution)/shard_map/all_to_all | solution.py:313
  8.8 46.8 %copy-start.1 = (bf16[176,1920]{1,0:T(8,128)(2,1)}, bf16[176,1920]{1,0:T(8,128)(2,1)S(1)}, u32[]{:S(2)}) copy-start(bf16[176,1920]{1,0:T(8,128)(2,1)S(1)} %concatenate.7.refs_0_) | copy-start | bytes 2027524
  8.8 22.4 %collective-permute-start.1 = (bf16[176,1920]{1,0:T(8,128)(2,1)S(1)}, bf16[176,1920]{1,0:T(8,128)(2,1)S(1)}, u32[]{:S(2)}, u32[]{:S(2)}) collective-permute-start(bf16[176,1920]{1,0:T(8,128)(2,1)S(1)} %concatenate.7.refs_0_), channel_id=1, source_target_pairs={{0,4},{4,0},{1,5},{5,1},{2,6},{6,2},{3,7},{7,3},{8,12},{12,8},{9,1... | collective-permute-start | bytes 2027528 | tf_op jit(solution)/shard_map/ppermute | solution.py:290
  12.2 19.3 %collective-permute-start.2 = (bf16[176,1920]{1,0:T(8,128)(2,1)S(1)}, bf16[176,1920]{1,0:T(8,128)(2,1)}, u32[]{:S(2)}, u32[]{:S(2)}) collective-permute-start(bf16[176,1920]{1,0:T(8,128)(2,1)S(1)} %concatenate.7.refs_0_), channel_id=1, source_target_pairs={{0,1},{1,2},{2,3},{3,0},{4,5},{5,6},{6,7},{7,4},{8,9},{9,10},{10,1... | collective-permute-start | bytes 2027528 | tf_op jit(solution)/shard_map/ppermute | solution.py:291
  15.3 18.8 %collective-permute-start.3 = (bf16[176,1920]{1,0:T(8,128)(2,1)S(1)}, bf16[176,1920]{1,0:T(8,128)(2,1)S(1)}, u32[]{:S(2)}, u32[]{:S(2)}) collective-permute-start(bf16[176,1920]{1,0:T(8,128)(2,1)S(1)} %concatenate.7.refs_0_), channel_id=1, source_target_pairs={{0,3},{1,0},{2,1},{3,2},{4,7},{5,4},{6,5},{7,6},{8,11},{9,8},{10,9... | collective-permute-start | bytes 2027528 | tf_op jit(solution)/shard_map/ppermute | solution.py:292
  18.7 36.9 %collective-permute-start = (bf16[832,512]{1,0:T(8,128)(2,1)S(1)}, bf16[832,512]{1,0:T(8,128)(2,1)}, u32[]{:S(2)}, u32[]{:S(2)}) collective-permute-start(bf16[832,512]{1,0:T(8,128)(2,1)S(1)} %bitcast.27), channel_id=1, source_target_pairs={{0,8},{8,0},{1,9},{9,1},{2,10},{10,2},{3,11},{11,3},{4,12},{12,4},... | collective-permute-start | bytes 2555912 | tf_op jit(solution)/shard_map/ppermute | solution.py:315
  31.3 0.9 copy-start.6
  34.1 0.8 copy-start.7
  35.0 13.5 %collective-permute-start.4 = (bf16[176,1920]{1,0:T(8,128)(2,1)}, bf16[176,1920]{1,0:T(8,128)(2,1)S(1)}, u32[]{:S(2)}, u32[]{:S(2)}) collective-permute-start(bf16[176,1920]{1,0:T(8,128)(2,1)} %collective-permute-done.2.refs_2_), channel_id=1, source_target_pairs={{0,4},{4,0},{1,5},{5,1},{2,6},{6,2},{3,7},{7,3},{8,12},{12,8},{9,1... | collective-permute-start | bytes 2027528 | tf_op jit(solution)/shard_map/ppermute | solution.py:296
  37.2 14.4 %collective-permute-start.5 = (bf16[176,1920]{1,0:T(8,128)(2,1)}, bf16[176,1920]{1,0:T(8,128)(2,1)S(1)}, u32[]{:S(2)}, u32[]{:S(2)}) collective-permute-start(bf16[176,1920]{1,0:T(8,128)(2,1)} %copy-done.6), channel_id=1, source_target_pairs={{0,3},{1,0},{2,1},{3,2},{4,7},{5,4},{6,5},{7,6},{8,11},{9,8},{10,9... | collective-permute-start | bytes 2027528 | tf_op jit(solution)/shard_map/ppermute | solution.py:297
  41.2 17.2 %collective-permute-start.6 = (bf16[176,1920]{1,0:T(8,128)(2,1)}, bf16[176,1920]{1,0:T(8,128)(2,1)}, u32[]{:S(2)}, u32[]{:S(2)}) collective-permute-start(bf16[176,1920]{1,0:T(8,128)(2,1)} %collective-permute-done.2.refs_2_), channel_id=1, source_target_pairs={{0,1},{1,2},{2,3},{3,0},{4,5},{5,6},{6,7},{7,4},{8,9},{9,10},{10,1... | collective-permute-start | bytes 2027528 | tf_op jit(solution)/shard_map/ppermute | solution.py:298
  48.5 7.1 %copy-start.4 = (bf16[176,1920]{1,0:T(8,128)(2,1)}, bf16[176,1920]{1,0:T(8,128)(2,1)S(1)}, u32[]{:S(2)}) copy-start(bf16[176,1920]{1,0:T(8,128)(2,1)S(1)} %collective-permute-done.4.refs_4_) | copy-start | bytes 2027524
  48.5 13.4 %collective-permute-start.7 = (bf16[80,1920]{1,0:T(8,128)(2,1)S(1)}, bf16[80,1920]{1,0:T(8,128)(2,1)S(1)}, u32[]{:S(2)}, u32[]{:S(2)}) collective-permute-start(bf16[80,1920]{1,0:T(8,128)(2,1)S(1)} %slice.40), channel_id=1, source_target_pairs={{0,1},{1,2},{2,3},{3,0},{4,5},{5,6},{6,7},{7,4},{8,9},{9,10},{10,1... | collective-permute-start | bytes 921608 | tf_op jit(solution)/shard_map/ppermute | solution.py:299
  51.6 4.0 %copy-start.3 = (bf16[176,1920]{1,0:T(8,128)(2,1)}, bf16[176,1920]{1,0:T(8,128)(2,1)S(1)}, u32[]{:S(2)}) copy-start(bf16[176,1920]{1,0:T(8,128)(2,1)S(1)} %collective-permute-done.5.refs_5_) | copy-start | bytes 2027524
  51.7 10.3 %collective-permute-start.8 = (bf16[96,1920]{1,0:T(8,128)(2,1)S(1)}, bf16[96,1920]{1,0:T(8,128)(2,1)S(1)}, u32[]{:S(2)}, u32[]{:S(2)}) collective-permute-start(bf16[96,1920]{1,0:T(8,128)(2,1)S(1)} %slice.41), channel_id=1, source_target_pairs={{0,3},{1,0},{2,1},{3,2},{4,7},{5,4},{6,5},{7,6},{8,11},{9,8},{10,9... | collective-permute-start | bytes 1105928 | tf_op jit(solution)/shard_map/ppermute | solution.py:300
  62.0 0.7 copy-start.9
  62.7 0.7 copy-start.8
  92.5 9.8 %collective-permute-start.9 = (bf16[128,512]{1,0:T(8,128)(2,1)}, bf16[128,512]{1,0:T(8,128)(2,1)S(1)}, u32[]{:S(2)}, u32[]{:S(2)}) collective-permute-start(bf16[128,512]{1,0:T(8,128)(2,1)} %get-tuple-element.17), channel_id=1, source_target_pairs={{0,8},{8,0},{1,9},{9,1},{2,10},{10,2},{3,11},{11,3},{4,12},{12,4},... | collective-permute-start | bytes 393224 | tf_op jit(solution)/shard_map/ppermute | solution.py:330
  102.3 0.7 copy-start.5
  104.8 37.9 %all-to-all-start.1 = ((bf16[48,16,128]{2,1,0:T(8,128)(2,1)}), bf16[48,16,128]{2,1,0:T(8,128)(2,1)S(1)}, u32[]{:S(2)}, u32[]{:S(2)}) async-start(bf16[48,16,128]{2,1,0:T(8,128)(2,1)} %tiles.1), calls=%async_computation.1 | async-start | bytes 393216 | tf_op jit(solution)/shard_map/all_to_all | solution.py:336
  143.5 21.2 %all-to-all-start.2 = ((bf16[48,16,128]{2,1,0:T(8,128)(2,1)}), bf16[48,16,128]{2,1,0:T(8,128)(2,1)S(1)}, u32[]{:S(2)}, u32[]{:S(2)}) async-start(bf16[48,16,128]{2,1,0:T(8,128)(2,1)} %reshape.115), calls=%async_computation.2 | async-start | bytes 393216 | tf_op jit(solution)/shard_map/all_to_all | solution.py:346

commit v4 on v3

--- a/solution.py
+++ b/solution.py
@@ -12,6 +12,7 @@
 LOG2E = 1.4426950408889634
 LN2 = 0.6931471805599453
 CHUNK = 128
+TALL = 352
 NT = (((1,), (1,)), ((), ()))
 TN = (((0,), (0,)), ((), ()))
 
@@ -42,16 +43,15 @@
     rows = group // n_fs
     padded = weight.shape[0]
     own = place_ref[0]
-    copies = []
+    copies, later = [pltpu.make_async_copy(weight_ref, weight.at[pl.ds(0, depth)], wsem)], []
     for k, (slot, down) in enumerate(layout):
         first = pl.multiple_of(place_ref[slot] * rows + down, 16)
         at = pl.ds(first, blocks[k].shape[0])
         source = blocks[k].at[:, pl.ds(width, padded)]
         copies.append(pltpu.make_async_copy(source, feats.at[at], fsem.at[k]))
         source = blocks[k].at[:, pl.ds(0, width)]
-        copies.append(pltpu.make_async_copy(source, words.at[at], tsem.at[k]))
-    copies.append(pltpu.make_async_copy(weight_ref, weight.at[pl.ds(0, depth)], wsem))
-    for copy in copies:
+        later.append(pltpu.make_async_copy(source, words.at[at], tsem.at[k]))
+    for copy in copies + later:
         copy.start()
     weight[depth:, :] = jnp.zeros((padded - depth, width), BF)
     dg[...] = jnp.zeros_like(dg)
@@ -63,20 +63,23 @@
             feats[...], weight[:, at : at + size], preferred_element_type=F32
         )
 
+    for copy in later:
+        copy.wait()
+
     def normalise(k, carry):
-        r = pl.ds(pl.multiple_of(k * CHUNK, CHUNK), CHUNK)
+        r = pl.ds(pl.multiple_of(k * TALL, TALL), TALL)
         z = u_full[r, :]
         inverse = lax.rsqrt(jnp.sum(z * z, axis=1, keepdims=True) + 1e-06)
         u = z * inverse
         u_full[r, :] = u
         unit[r, :] = u.astype(BF)
-        inv_u[r, :] = jnp.broadcast_to(inverse, (CHUNK, 128))
+        inv_u[r, :] = jnp.broadcast_to(inverse, (TALL, 128))
         t = words[r, :].astype(F32)
         inverse = lax.rsqrt(jnp.sum(t * t, axis=1, keepdims=True) + 1e-06)
         text[r, :] = (t * inverse).astype(BF)
         return carry
 
-    lax.fori_loop(0, group // CHUNK, normalise, 0)
+    lax.fori_loop(0, group // TALL, normalise, 0, unroll=True)
     out_unit = pltpu.make_async_copy(unit, unit_out, osem.at[0])
     out_unit.start()
 
@@ -116,6 +119,7 @@
         group // CHUNK,
         by_row,
         (jnp.full((8, group), -jnp.inf, F32), jnp.zeros((CHUNK, 1), F32)),
+        unroll=True,
     )
     peak = jnp.max(peak, axis=0, keepdims=True)
 
@@ -150,14 +154,14 @@
         )
 
     def to_dz(k, carry):
-        r = pl.ds(pl.multiple_of(k * CHUNK, CHUNK), CHUNK)
+        r = pl.ds(pl.multiple_of(k * TALL, TALL), TALL)
         du = 100.0 * prob[r, :width]
         u = u_full[r, :]
         along = jnp.sum(u * du, axis=1, keepdims=True)
         dz[r, :] = ((du - u * along) * inv_u[r, 0:1]).astype(BF)
         return carry
 
-    lax.fori_loop(0, group // CHUNK, to_dz, 0)
+    lax.fori_loop(0, group // TALL, to_dz, 0, unroll=True)
     mine = dz.at[pl.ds(pl.multiple_of(own * rows, 16), rows)]
     out_dz = pltpu.make_async_copy(mine, dz_out, osem.at[2])
     out_dz.start()
@@ -303,15 +307,13 @@
     return keys, list(got.values()) + [low, high], layout, got
 
 
-def whole_head(head_weight, part, n_fs, first, later):
+def whole_head(head_weight, part, n_fs):
     rows, width = head_weight.shape
     half = width // 2
     core = lax.axis_index("core")
     mine = jnp.where(core == 0, head_weight[:, :half], head_weight[:, half:])
-    mine = lax.optimization_barrier((mine, *first))[0]
     mine = jnp.broadcast_to(mine[None], (n_fs, rows, half))
     mine = lax.all_to_all(mine, part, 0, 0, tiled=True).reshape(n_fs * rows, half)
-    mine = lax.optimization_barrier((mine, *later))[0]
     other = lax.ppermute(mine, "core", [(0, 1), (1, 0)])
     left = jnp.where(core == 0, mine, other)
     right = jnp.where(core == 0, other, mine)
@@ -370,7 +372,7 @@
         keys, blocks, layout, got = gather_group(packed, n_y, n_x)
         place = [((y + dy) % n_y) * n_x + (x + dx) % n_x for dy, dx in keys]
         place = jnp.stack(place + [lax.axis_index("core")]).astype(jnp.int32)
-        weight = whole_head(head_weight, part, n_fs, [], [])
+        weight = whole_head(head_weight, part, n_fs)
         mine, other, loss, image_unit, coupling, dz = group_call(
             place, weight, blocks, tuple(layout)
         )

time: 174 us -> 170 us (0.977)
  Pallas kernels: 30.9 us -> 26.9 us
    pallas_call x1, Pallas kernels: 29.1 us -> 25.1 us  [group_call(): pl.pallas_call(functools.partial(group_kernel, n_fs, depth, layout), out_...]
where the time goes in v4:
time: 170 us; the launch traced here: 169 us
  starting transfers between devices  79.1 us (47%)
  waiting for transfers between devices  36.6 us (22%)
  Pallas kernels  26.9 us (16%)
  other arithmetic  6.46 us (4%)
  local copies, waits for them, and re-layouts  6.3 us (4%)
  matrix products  5.77 us (3%)
  blocking collectives  5.3 us (3%)
  between operations  2.8 us (2%)
    pallas_call x1, Pallas kernels, group_call(): pl.pallas_call(functools.partial(group_kernel, n_fs, depth, layout), out_...  25.1 us
    all_to_all x1, starting transfers between devices, sum_over_groups(): tiles = lax.all_to_all(tiles, ('yh', 'z'), 0, 0, tiled=True)  21.4 us
    all_to_all x1, waiting for transfers between devices, sum_over_groups(): tiles = lax.all_to_all(tiles, ('yh', 'z'), 0, 0, tiled=True)  14 us
    ppermute x1, starting transfers between devices, whole_head(): other = lax.ppermute(mine, 'core', [(0, 1), (1, 0)])  12.5 us
    all_to_all x1, waiting for transfers between devices, sum_over_groups(): tiles = lax.all_to_all(send, ('yh', 'z'), 0, 0, tiled=True)  11.2 us
    ppermute x1, starting transfers between devices, sum_over_groups(): came = lax.ppermute(other, 'core', [(0, 1), (1, 0)])  8.62 us
    all_to_all x1, starting transfers between devices, whole_head(): lax.all_to_all(mine, part, 0, 0, tiled=True).reshape(n_fs * rows, half)  5.86 us
    all_to_all x1, starting transfers between devices, sum_over_groups(): tiles = lax.all_to_all(send, ('yh', 'z'), 0, 0, tiled=True)  5.67 us
  transfers between devices with their start and end apart: 13, of which 7 were waited for; matrix products, arithmetic and copies ran while one was open for 6% of the time, Pallas kernels for 0%

profile of v4, /device:TPU:1, one launch (start us, length us, event | category | flops | bytes accessed | tf_op | source)
XLA Modules:
  0.0 169.3 jit_solution(15814589189754535579)
XLA Ops:
  0.7 1.0 slice_select_fusion
  1.7 1.0 broadcast_in_dim.32
  2.6 5.9 %all-to-all-start = ((bf16[8,104,512]{2,1,0:T(8,128)(2,1)}), bf16[8,104,512]{2,1,0:T(8,128)(2,1)S(1)}, u32[]{:S(2)}, u32[]{:S(2)}) async-start(bf16[8,104,512]{2,1,0:T(8,128)(2,1)} %broadcast_in_dim.32), calls=%async_computation | async-start | bytes 1703936 | tf_op jit(solution)/shard_map/all_to_all | solution.py:316
  8.5 0.3 concatenate.7.refs_0_
  8.8 3.4 %collective-permute-start.1 = (bf16[176,1920]{1,0:T(8,128)(2,1)S(1)}, bf16[176,1920]{1,0:T(8,128)(2,1)S(1)}, u32[]{:S(2)}, u32[]{:S(2)}) collective-permute-start(bf16[176,1920]{1,0:T(8,128)(2,1)S(1)} %concatenate.7.refs_0_), channel_id=1, source_target_pairs={{0,4},{4,0},{1,5},{5,1},{2,6},{6,2},{3,7},{7,3},{8,12},{12,8},{9,1... | collective-permute-start | bytes 2027528 | tf_op jit(solution)/shard_map/ppermute | solution.py:294
  12.2 3.1 %collective-permute-start.2 = (bf16[176,1920]{1,0:T(8,128)(2,1)S(1)}, bf16[176,1920]{1,0:T(8,128)(2,1)}, u32[]{:S(2)}, u32[]{:S(2)}) collective-permute-start(bf16[176,1920]{1,0:T(8,128)(2,1)S(1)} %concatenate.7.refs_0_), channel_id=1, source_target_pairs={{0,1},{1,2},{2,3},{3,0},{4,5},{5,6},{6,7},{7,4},{8,9},{9,10},{10,1... | collective-permute-start | bytes 2027528 | tf_op jit(solution)/shard_map/ppermute | solution.py:295
  15.3 3.4 %collective-permute-start.3 = (bf16[176,1920]{1,0:T(8,128)(2,1)S(1)}, bf16[176,1920]{1,0:T(8,128)(2,1)S(1)}, u32[]{:S(2)}, u32[]{:S(2)}) collective-permute-start(bf16[176,1920]{1,0:T(8,128)(2,1)S(1)} %concatenate.7.refs_0_), channel_id=1, source_target_pairs={{0,3},{1,0},{2,1},{3,2},{4,7},{5,4},{6,5},{7,6},{8,11},{9,8},{10,9... | collective-permute-start | bytes 2027528 | tf_op jit(solution)/shard_map/ppermute | solution.py:296
  18.7 0.0 all-to-all-done
  18.7 12.5 %collective-permute-start = (bf16[832,512]{1,0:T(8,128)(2,1)S(1)}, bf16[832,512]{1,0:T(8,128)(2,1)}, u32[]{:S(2)}, u32[]{:S(2)}) collective-permute-start(bf16[832,512]{1,0:T(8,128)(2,1)S(1)} %bitcast.29), channel_id=1, source_target_pairs={{0,8},{8,0},{1,9},{9,1},{2,10},{10,2},{3,11},{11,3},{4,12},{12,4},... | collective-permute-start | bytes 2555912 | tf_op jit(solution)/shard_map/ppermute | solution.py:317
  31.3 0.0 collective-permute-done.1.refs_1_
  31.3 0.3 collective-permute-done.2.refs_2_
  31.6 0.6 copy-done.6
  32.2 2.0 %collective-permute-done.3.refs_3_ = bf16[176,1920]{1,0:T(8,128)(2,1)S(1)} collective-permute-done((bf16[176,1920]{1,0:T(8,128)(2,1)S(1)}, bf16[176,1920]{1,0:T(8,128)(2,1)S(1)}, u32[]{:S(2)}, u32[]{:S(2)}) %collective-permute-start.3) | collective-permute-done | bytes 675872 | tf_op jit(solution)/shard_map/ppermute | solution.py:296
  34.1 0.8 copy-done.7
  35.0 2.2 %collective-permute-start.4 = (bf16[176,1920]{1,0:T(8,128)(2,1)}, bf16[176,1920]{1,0:T(8,128)(2,1)S(1)}, u32[]{:S(2)}, u32[]{:S(2)}) collective-permute-start(bf16[176,1920]{1,0:T(8,128)(2,1)} %collective-permute-done.2.refs_2_), channel_id=1, source_target_pairs={{0,4},{4,0},{1,5},{5,1},{2,6},{6,2},{3,7},{7,3},{8,12},{12,8},{9,1... | collective-permute-start | bytes 2027528 | tf_op jit(solution)/shard_map/ppermute | solution.py:300
  37.2 4.0 %collective-permute-start.5 = (bf16[176,1920]{1,0:T(8,128)(2,1)}, bf16[176,1920]{1,0:T(8,128)(2,1)S(1)}, u32[]{:S(2)}, u32[]{:S(2)}) collective-permute-start(bf16[176,1920]{1,0:T(8,128)(2,1)} %copy-done.6), channel_id=1, source_target_pairs={{0,3},{1,0},{2,1},{3,2},{4,7},{5,4},{6,5},{7,6},{8,11},{9,8},{10,9... | collective-permute-start | bytes 2027528 | tf_op jit(solution)/shard_map/ppermute | solution.py:301
  41.2 1.9 %collective-permute-start.6 = (bf16[176,1920]{1,0:T(8,128)(2,1)}, bf16[176,1920]{1,0:T(8,128)(2,1)}, u32[]{:S(2)}, u32[]{:S(2)}) collective-permute-start(bf16[176,1920]{1,0:T(8,128)(2,1)} %collective-permute-done.2.refs_2_), channel_id=1, source_target_pairs={{0,1},{1,2},{2,3},{3,0},{4,5},{5,6},{6,7},{7,4},{8,9},{9,10},{10,1... | collective-permute-start | bytes 2027528 | tf_op jit(solution)/shard_map/ppermute | solution.py:302
  43.2 0.6 stack.39.place_ref
  43.8 4.7 %collective-permute-done.4.refs_4_ = bf16[176,1920]{1,0:T(8,128)(2,1)S(1)} collective-permute-done((bf16[176,1920]{1,0:T(8,128)(2,1)}, bf16[176,1920]{1,0:T(8,128)(2,1)S(1)}, u32[]{:S(2)}, u32[]{:S(2)}) %collective-permute-start.4) | collective-permute-done | bytes 675872 | tf_op jit(solution)/shard_map/ppermute | solution.py:300
  48.5 3.1 %collective-permute-start.7 = (bf16[80,1920]{1,0:T(8,128)(2,1)S(1)}, bf16[80,1920]{1,0:T(8,128)(2,1)S(1)}, u32[]{:S(2)}, u32[]{:S(2)}) collective-permute-start(bf16[80,1920]{1,0:T(8,128)(2,1)S(1)} %slice.40), channel_id=1, source_target_pairs={{0,1},{1,2},{2,3},{3,0},{4,5},{5,6},{6,7},{7,4},{8,9},{9,10},{10,1... | collective-permute-start | bytes 921608 | tf_op jit(solution)/shard_map/ppermute | solution.py:303
  51.6 0.0 collective-permute-done.5.refs_5_
  51.7 3.9 %collective-permute-start.8 = (bf16[96,1920]{1,0:T(8,128)(2,1)S(1)}, bf16[96,1920]{1,0:T(8,128)(2,1)S(1)}, u32[]{:S(2)}, u32[]{:S(2)}) collective-permute-start(bf16[96,1920]{1,0:T(8,128)(2,1)S(1)} %slice.41), channel_id=1, source_target_pairs={{0,3},{1,0},{2,1},{3,2},{4,7},{5,4},{6,5},{7,6},{8,11},{9,8},{10,9... | collective-permute-start | bytes 1105928 | tf_op jit(solution)/shard_map/ppermute | solution.py:304
  55.6 0.0 collective-permute-done
  55.7 1.3 broadcast_select_fusion.1
  56.9 1.5 pad_maximum_fusion.weight_ref
  58.4 3.6 %collective-permute-done.7.refs_7_ = bf16[80,1920]{1,0:T(8,128)(2,1)S(1)} collective-permute-done((bf16[80,1920]{1,0:T(8,128)(2,1)S(1)}, bf16[80,1920]{1,0:T(8,128)(2,1)S(1)}, u32[]{:S(2)}, u32[]{:S(2)}) %collective-permute-start.7) | collective-permute-done | bytes 307232 | tf_op jit(solution)/shard_map/ppermute | solution.py:303
  62.0 0.0 collective-permute-done.8.refs_8_
  62.0 0.7 copy-done.9
  62.7 0.7 copy-done.8
  63.4 25.1 %group.1 = (f32[112,512]{1,0:T(8,128)}, bf16[128,512]{1,0:T(8,128)(2,1)}, f32[8,128]{1,0:T(8,128)}, bf16[1408,1024]{1,0:T(8,128)(2,1)}, bf16[1408,1408]{1,0:T(8,128)(2,1)}, /*index=5*/bf16[176,1024]{1,0:T(8,128)(2,1)}) custom-call(s32[9]{0:T(128)} %stack.39.place_ref, bf16[832,1024]{1,0:T(8,128)(2,1)} %pad_maximum_fusion.weight_ref, ...), custom_call_target="tpu_custom_call" | custom-call | flops 12000000000 | bytes 20000000 | tf_op jit(solution)/shard_map/group/pallas_call | solution.py:202
  88.6 8.6 %collective-permute-start.9 = (bf16[128,512]{1,0:T(8,128)(2,1)}, bf16[128,512]{1,0:T(8,128)(2,1)S(1)}, u32[]{:S(2)}, u32[]{:S(2)}) collective-permute-start(bf16[128,512]{1,0:T(8,128)(2,1)} %get-tuple-element.17), channel_id=1, source_target_pairs={{0,8},{8,0},{1,9},{9,1},{2,10},{10,2},{3,11},{11,3},{4,12},{12,4},... | collective-permute-start | bytes 393224 | tf_op jit(solution)/shard_map/ppermute | solution.py:332
  97.2 0.2 fusion.6
  97.4 1.0 collective-permute-done.9.came_ref
  98.4 0.7 copy-done.5
  99.0 1.8 %tiles.1 = bf16[48,16,128]{2,1,0:T(8,128)(2,1)} custom-call(f32[112,512]{1,0:T(8,128)} %get-tuple-element.16.mine_ref, bf16[128,512]{1,0:T(8,128)(2,1)} %copy-done.5, f32[8,128]{1,0:T(8,128)} %get-tuple-element.18.loss_ref), custom_call_target="tpu_custom_call" | custom-call | tf_op jit(solution)/shard_map/tiles/pallas_call | solution.py:258
  100.8 21.4 %all-to-all-start.1 = ((bf16[48,16,128]{2,1,0:T(8,128)(2,1)}), bf16[48,16,128]{2,1,0:T(8,128)(2,1)S(1)}, u32[]{:S(2)}, u32[]{:S(2)}) async-start(bf16[48,16,128]{2,1,0:T(8,128)(2,1)} %tiles.1), calls=%async_computation.1 | async-start | bytes 393216 | tf_op jit(solution)/shard_map/all_to_all | solution.py:338
  122.3 2.5 %convolution_convert_fusion = bf16[176,832]{1,0:T(8,128)(2,1)} fusion(bf16[176,1024]{1,0:T(8,128)(2,1)} %get-tuple-element.19, bf16[832,512]{1,0:T(8,128)(2,1)S(1)} %get-tuple-element.23, bf16[832,512]{1,0:T(8,128)(2,1)S(1)} %get-tuple-element.22), kind=kOutput, calls=%fused_computation.2 | convolution fusion | flops 303447040 | bytes 2357248 | tf_op jit(solution)/shard_map/dot_general | solution.py:275
  124.8 14.0 %all-to-all-done.1 = bf16[48,16,128]{2,1,0:T(8,128)(2,1)S(1)} async-done(((bf16[48,16,128]{2,1,0:T(8,128)(2,1)}), bf16[48,16,128]{2,1,0:T(8,128)(2,1)S(1)}, u32[]{:S(2)}, u32[]{:S(2)}) %all-to-all-start.1) | async-done | bytes 196640 | tf_op jit(solution)/shard_map/all_to_all | solution.py:338
  138.7 0.1 convert_reduce_fusion
  138.8 0.1 select_select_fusion
  138.9 0.7 reshape.115
  139.6 5.7 %all-to-all-start.2 = ((bf16[48,16,128]{2,1,0:T(8,128)(2,1)}), bf16[48,16,128]{2,1,0:T(8,128)(2,1)S(1)}, u32[]{:S(2)}, u32[]{:S(2)}) async-start(bf16[48,16,128]{2,1,0:T(8,128)(2,1)} %reshape.115), calls=%async_computation.2 | async-start | bytes 393216 | tf_op jit(solution)/shard_map/all_to_all | solution.py:348
  145.2 3.3 %fusion.2 = (f32[176]{0:T(256)S(1)}, f32[176,1024]{1,0:T(8,128)S(1)}) fusion(bf16[176,1024]{1,0:T(8,128)(2,1)S(1)} %copy-done, f32[176]{0:T(256)S(1)} %add_rsqrt_fusion, bf16[1408,1024]{1,0:T(8,128)(2,1)} %get-tuple-element.21, bf16[1408,1408]{1,0:T(8,128)(2,1)} %get-tuple-element.20, s32[]{:T(128)S(6)} %select_n.102), kind=kOutput, calls=%fused_computation.9 | convolution fusion | flops 508411712 | bytes 4687236 | tf_op jit(solution)/shard_map/dot_general | solution.py:269
  148.5 1.0 fusion.5
  149.5 11.2 %all-to-all-done.2 = bf16[48,16,128]{2,1,0:T(8,128)(2,1)S(1)} async-done(((bf16[48,16,128]{2,1,0:T(8,128)(2,1)}), bf16[48,16,128]{2,1,0:T(8,128)(2,1)S(1)}, u32[]{:S(2)}, u32[]{:S(2)}) %all-to-all-start.2) | async-done | bytes 196640 | tf_op jit(solution)/shard_map/all_to_all | solution.py:348
  160.8 5.3 %all_gather.3 = bf16[112,1024]{1,0:T(8,128)(2,1)S(1)} all-gather(bf16[112,512]{1,0:T(8,128)(2,1)S(1)} %bitcast.32), channel_id=1, replica_groups=mesh['yh'=4,'z'=12,'core'=2,'yl'=2,'x'=4] {'core'}, dimensions={1}, use_global_device_ids=true | all-gather | bytes 344064 | tf_op jit(solution)/shard_map/all_gather | solution.py:352
  166.1 0.8 slice_convert_fusion
  166.9 0.6 convert_reduce_fusion.1
  (26 shorter events, 0.2 us)
Async XLA Ops:
  0.6 7.9 %copy-start.2 = (bf16[176,832]{1,0:T(8,128)(2,1)S(1)}, bf16[176,832]{1,0:T(8,128)(2,1)}, u32[]{:S(2)}) copy-start(bf16[176,832]{1,0:T(8,128)(2,1)} %param.3) | copy-start | bytes 878596
  0.6 7.9 %copy-start = (bf16[176,1024]{1,0:T(8,128)(2,1)S(1)}, bf16[176,1024]{1,0:T(8,128)(2,1)}, u32[]{:S(2)}) copy-start(bf16[176,1024]{1,0:T(8,128)(2,1)} %param.5) | copy-start | bytes 1081348
  2.6 16.1 %all-to-all-start = ((bf16[8,104,512]{2,1,0:T(8,128)(2,1)}), bf16[8,104,512]{2,1,0:T(8,128)(2,1)S(1)}, u32[]{:S(2)}, u32[]{:S(2)}) async-start(bf16[8,104,512]{2,1,0:T(8,128)(2,1)} %broadcast_in_dim.32), calls=%async_computation | async-start | bytes 1703936 | tf_op jit(solution)/shard_map/all_to_all | solution.py:316
  8.8 46.8 %copy-start.1 = (bf16[176,1920]{1,0:T(8,128)(2,1)}, bf16[176,1920]{1,0:T(8,128)(2,1)S(1)}, u32[]{:S(2)}) copy-start(bf16[176,1920]{1,0:T(8,128)(2,1)S(1)} %concatenate.7.refs_0_) | copy-start | bytes 2027524
  8.8 22.4 %collective-permute-start.1 = (bf16[176,1920]{1,0:T(8,128)(2,1)S(1)}, bf16[176,1920]{1,0:T(8,128)(2,1)S(1)}, u32[]{:S(2)}, u32[]{:S(2)}) collective-permute-start(bf16[176,1920]{1,0:T(8,128)(2,1)S(1)} %concatenate.7.refs_0_), channel_id=1, source_target_pairs={{0,4},{4,0},{1,5},{5,1},{2,6},{6,2},{3,7},{7,3},{8,12},{12,8},{9,1... | collective-permute-start | bytes 2027528 | tf_op jit(solution)/shard_map/ppermute | solution.py:294
  12.2 19.3 %collective-permute-start.2 = (bf16[176,1920]{1,0:T(8,128)(2,1)S(1)}, bf16[176,1920]{1,0:T(8,128)(2,1)}, u32[]{:S(2)}, u32[]{:S(2)}) collective-permute-start(bf16[176,1920]{1,0:T(8,128)(2,1)S(1)} %concatenate.7.refs_0_), channel_id=1, source_target_pairs={{0,1},{1,2},{2,3},{3,0},{4,5},{5,6},{6,7},{7,4},{8,9},{9,10},{10,1... | collective-permute-start | bytes 2027528 | tf_op jit(solution)/shard_map/ppermute | solution.py:295
  15.3 18.8 %collective-permute-start.3 = (bf16[176,1920]{1,0:T(8,128)(2,1)S(1)}, bf16[176,1920]{1,0:T(8,128)(2,1)S(1)}, u32[]{:S(2)}, u32[]{:S(2)}) collective-permute-start(bf16[176,1920]{1,0:T(8,128)(2,1)S(1)} %concatenate.7.refs_0_), channel_id=1, source_target_pairs={{0,3},{1,0},{2,1},{3,2},{4,7},{5,4},{6,5},{7,6},{8,11},{9,8},{10,9... | collective-permute-start | bytes 2027528 | tf_op jit(solution)/shard_map/ppermute | solution.py:296
  18.7 36.9 %collective-permute-start = (bf16[832,512]{1,0:T(8,128)(2,1)S(1)}, bf16[832,512]{1,0:T(8,128)(2,1)}, u32[]{:S(2)}, u32[]{:S(2)}) collective-permute-start(bf16[832,512]{1,0:T(8,128)(2,1)S(1)} %bitcast.29), channel_id=1, source_target_pairs={{0,8},{8,0},{1,9},{9,1},{2,10},{10,2},{3,11},{11,3},{4,12},{12,4},... | collective-permute-start | bytes 2555912 | tf_op jit(solution)/shard_map/ppermute | solution.py:317
  31.3 0.9 copy-start.6
  34.1 0.8 copy-start.7
  35.0 13.5 %collective-permute-start.4 = (bf16[176,1920]{1,0:T(8,128)(2,1)}, bf16[176,1920]{1,0:T(8,128)(2,1)S(1)}, u32[]{:S(2)}, u32[]{:S(2)}) collective-permute-start(bf16[176,1920]{1,0:T(8,128)(2,1)} %collective-permute-done.2.refs_2_), channel_id=1, source_target_pairs={{0,4},{4,0},{1,5},{5,1},{2,6},{6,2},{3,7},{7,3},{8,12},{12,8},{9,1... | collective-permute-start | bytes 2027528 | tf_op jit(solution)/shard_map/ppermute | solution.py:300
  37.2 14.4 %collective-permute-start.5 = (bf16[176,1920]{1,0:T(8,128)(2,1)}, bf16[176,1920]{1,0:T(8,128)(2,1)S(1)}, u32[]{:S(2)}, u32[]{:S(2)}) collective-permute-start(bf16[176,1920]{1,0:T(8,128)(2,1)} %copy-done.6), channel_id=1, source_target_pairs={{0,3},{1,0},{2,1},{3,2},{4,7},{5,4},{6,5},{7,6},{8,11},{9,8},{10,9... | collective-permute-start | bytes 2027528 | tf_op jit(solution)/shard_map/ppermute | solution.py:301
  41.2 17.2 %collective-permute-start.6 = (bf16[176,1920]{1,0:T(8,128)(2,1)}, bf16[176,1920]{1,0:T(8,128)(2,1)}, u32[]{:S(2)}, u32[]{:S(2)}) collective-permute-start(bf16[176,1920]{1,0:T(8,128)(2,1)} %collective-permute-done.2.refs_2_), channel_id=1, source_target_pairs={{0,1},{1,2},{2,3},{3,0},{4,5},{5,6},{6,7},{7,4},{8,9},{9,10},{10,1... | collective-permute-start | bytes 2027528 | tf_op jit(solution)/shard_map/ppermute | solution.py:302
  48.5 7.1 %copy-start.4 = (bf16[176,1920]{1,0:T(8,128)(2,1)}, bf16[176,1920]{1,0:T(8,128)(2,1)S(1)}, u32[]{:S(2)}) copy-start(bf16[176,1920]{1,0:T(8,128)(2,1)S(1)} %collective-permute-done.4.refs_4_) | copy-start | bytes 2027524
  48.5 13.4 %collective-permute-start.7 = (bf16[80,1920]{1,0:T(8,128)(2,1)S(1)}, bf16[80,1920]{1,0:T(8,128)(2,1)S(1)}, u32[]{:S(2)}, u32[]{:S(2)}) collective-permute-start(bf16[80,1920]{1,0:T(8,128)(2,1)S(1)} %slice.40), channel_id=1, source_target_pairs={{0,1},{1,2},{2,3},{3,0},{4,5},{5,6},{6,7},{7,4},{8,9},{9,10},{10,1... | collective-permute-start | bytes 921608 | tf_op jit(solution)/shard_map/ppermute | solution.py:303
  51.6 4.0 %copy-start.3 = (bf16[176,1920]{1,0:T(8,128)(2,1)}, bf16[176,1920]{1,0:T(8,128)(2,1)S(1)}, u32[]{:S(2)}) copy-start(bf16[176,1920]{1,0:T(8,128)(2,1)S(1)} %collective-permute-done.5.refs_5_) | copy-start | bytes 2027524
  51.7 10.3 %collective-permute-start.8 = (bf16[96,1920]{1,0:T(8,128)(2,1)S(1)}, bf16[96,1920]{1,0:T(8,128)(2,1)S(1)}, u32[]{:S(2)}, u32[]{:S(2)}) collective-permute-start(bf16[96,1920]{1,0:T(8,128)(2,1)S(1)} %slice.41), channel_id=1, source_target_pairs={{0,3},{1,0},{2,1},{3,2},{4,7},{5,4},{6,5},{7,6},{8,11},{9,8},{10,9... | collective-permute-start | bytes 1105928 | tf_op jit(solution)/shard_map/ppermute | solution.py:304
  62.0 0.7 copy-start.9
  62.7 0.7 copy-start.8
  88.6 9.8 %collective-permute-start.9 = (bf16[128,512]{1,0:T(8,128)(2,1)}, bf16[128,512]{1,0:T(8,128)(2,1)S(1)}, u32[]{:S(2)}, u32[]{:S(2)}) collective-permute-start(bf16[128,512]{1,0:T(8,128)(2,1)} %get-tuple-element.17), channel_id=1, source_target_pairs={{0,8},{8,0},{1,9},{9,1},{2,10},{10,2},{3,11},{11,3},{4,12},{12,4},... | collective-permute-start | bytes 393224 | tf_op jit(solution)/shard_map/ppermute | solution.py:332
  98.4 0.7 copy-start.5
  100.8 37.9 %all-to-all-start.1 = ((bf16[48,16,128]{2,1,0:T(8,128)(2,1)}), bf16[48,16,128]{2,1,0:T(8,128)(2,1)S(1)}, u32[]{:S(2)}, u32[]{:S(2)}) async-start(bf16[48,16,128]{2,1,0:T(8,128)(2,1)} %tiles.1), calls=%async_computation.1 | async-start | bytes 393216 | tf_op jit(solution)/shard_map/all_to_all | solution.py:338
  139.6 21.2 %all-to-all-start.2 = ((bf16[48,16,128]{2,1,0:T(8,128)(2,1)}), bf16[48,16,128]{2,1,0:T(8,128)(2,1)S(1)}, u32[]{:S(2)}, u32[]{:S(2)}) async-start(bf16[48,16,128]{2,1,0:T(8,128)(2,1)} %reshape.115), calls=%async_computation.2 | async-start | bytes 393216 | tf_op jit(solution)/shard_map/all_to_all | solution.py:348

commit v5 on v4

--- a/solution.py
+++ b/solution.py
@@ -129,7 +129,9 @@
         score[r, :] = q
         return total + jnp.sum(tiles(q), axis=0)
 
-    total = lax.fori_loop(0, group // CHUNK, by_col, jnp.zeros((8, group), F32))
+    total = lax.fori_loop(
+        0, group // CHUNK, by_col, jnp.zeros((8, group), F32), unroll=True
+    )
     total = jnp.sum(total, axis=0, keepdims=True)
     col_terms = peak + jnp.log2(total) - jnp.sum(dg[...], axis=0, keepdims=True)
     loss = LN2 * (jnp.sum(row_terms) + jnp.sum(col_terms))
@@ -144,7 +146,7 @@
         coupling[r, cols] = (c - jnp.where(eye, 2.0, 0.0)).astype(BF)
         return carry
 
-    lax.fori_loop(0, group // CHUNK, couple, 0)
+    lax.fori_loop(0, group // CHUNK, couple, 0, unroll=True)
     out_coupling = pltpu.make_async_copy(coupling, coupling_out, osem.at[1])
     out_coupling.start()
 

time: 170 us -> 169 us (level)
  no operation moved by 1% of the time
where the time goes in v5:
time: 169 us; the launch traced here: 168 us
  starting transfers between devices  79.1 us (47%)
  waiting for transfers between devices  36.7 us (22%)
  Pallas kernels  25.6 us (15%)
  other arithmetic  6.46 us (4%)
  local copies, waits for them, and re-layouts  6.3 us (4%)
  matrix products  5.74 us (3%)
  blocking collectives  5.3 us (3%)
  between operations  2.8 us (2%)
    pallas_call x1, Pallas kernels, group_call(): pl.pallas_call(functools.partial(group_kernel, n_fs, depth, layout), out_...  23.8 us
    all_to_all x1, starting transfers between devices, sum_over_groups(): tiles = lax.all_to_all(tiles, ('yh', 'z'), 0, 0, tiled=True)  21.4 us
    all_to_all x1, waiting for transfers between devices, sum_over_groups(): tiles = lax.all_to_all(tiles, ('yh', 'z'), 0, 0, tiled=True)  14 us
    ppermute x1, starting transfers between devices, whole_head(): other = lax.ppermute(mine, 'core', [(0, 1), (1, 0)])  12.5 us
    all_to_all x1, waiting for transfers between devices, sum_over_groups(): tiles = lax.all_to_all(send, ('yh', 'z'), 0, 0, tiled=True)  11.2 us
    ppermute x1, starting transfers between devices, sum_over_groups(): came = lax.ppermute(other, 'core', [(0, 1), (1, 0)])  8.62 us
    all_to_all x1, starting transfers between devices, whole_head(): lax.all_to_all(mine, part, 0, 0, tiled=True).reshape(n_fs * rows, half)  5.86 us
    all_to_all x1, starting transfers between devices, sum_over_groups(): tiles = lax.all_to_all(send, ('yh', 'z'), 0, 0, tiled=True)  5.67 us
  transfers between devices with their start and end apart: 13, of which 7 were waited for; matrix products, arithmetic and copies ran while one was open for 6% of the time, Pallas kernels for 0%

profile of v5, /device:TPU:1, one launch (start us, length us, event | category | flops | bytes accessed | tf_op | source)
XLA Modules:
  0.0 168.0 jit_solution(5390422033327366338)
XLA Ops:
  0.7 1.0 slice_select_fusion
  1.7 1.0 broadcast_in_dim.32
  2.6 5.9 %all-to-all-start = ((bf16[8,104,512]{2,1,0:T(8,128)(2,1)}), bf16[8,104,512]{2,1,0:T(8,128)(2,1)S(1)}, u32[]{:S(2)}, u32[]{:S(2)}) async-start(bf16[8,104,512]{2,1,0:T(8,128)(2,1)} %broadcast_in_dim.32), calls=%async_computation | async-start | bytes 1703936 | tf_op jit(solution)/shard_map/all_to_all | solution.py:318
  8.5 0.3 concatenate.7.refs_0_
  8.8 3.4 %collective-permute-start.1 = (bf16[176,1920]{1,0:T(8,128)(2,1)S(1)}, bf16[176,1920]{1,0:T(8,128)(2,1)S(1)}, u32[]{:S(2)}, u32[]{:S(2)}) collective-permute-start(bf16[176,1920]{1,0:T(8,128)(2,1)S(1)} %concatenate.7.refs_0_), channel_id=1, source_target_pairs={{0,4},{4,0},{1,5},{5,1},{2,6},{6,2},{3,7},{7,3},{8,12},{12,8},{9,1... | collective-permute-start | bytes 2027528 | tf_op jit(solution)/shard_map/ppermute | solution.py:296
  12.2 3.1 %collective-permute-start.2 = (bf16[176,1920]{1,0:T(8,128)(2,1)S(1)}, bf16[176,1920]{1,0:T(8,128)(2,1)}, u32[]{:S(2)}, u32[]{:S(2)}) collective-permute-start(bf16[176,1920]{1,0:T(8,128)(2,1)S(1)} %concatenate.7.refs_0_), channel_id=1, source_target_pairs={{0,1},{1,2},{2,3},{3,0},{4,5},{5,6},{6,7},{7,4},{8,9},{9,10},{10,1... | collective-permute-start | bytes 2027528 | tf_op jit(solution)/shard_map/ppermute | solution.py:297
  15.3 3.4 %collective-permute-start.3 = (bf16[176,1920]{1,0:T(8,128)(2,1)S(1)}, bf16[176,1920]{1,0:T(8,128)(2,1)S(1)}, u32[]{:S(2)}, u32[]{:S(2)}) collective-permute-start(bf16[176,1920]{1,0:T(8,128)(2,1)S(1)} %concatenate.7.refs_0_), channel_id=1, source_target_pairs={{0,3},{1,0},{2,1},{3,2},{4,7},{5,4},{6,5},{7,6},{8,11},{9,8},{10,9... | collective-permute-start | bytes 2027528 | tf_op jit(solution)/shard_map/ppermute | solution.py:298
  18.7 0.0 all-to-all-done
  18.7 12.5 %collective-permute-start = (bf16[832,512]{1,0:T(8,128)(2,1)S(1)}, bf16[832,512]{1,0:T(8,128)(2,1)}, u32[]{:S(2)}, u32[]{:S(2)}) collective-permute-start(bf16[832,512]{1,0:T(8,128)(2,1)S(1)} %bitcast.29), channel_id=1, source_target_pairs={{0,8},{8,0},{1,9},{9,1},{2,10},{10,2},{3,11},{11,3},{4,12},{12,4},... | collective-permute-start | bytes 2555912 | tf_op jit(solution)/shard_map/ppermute | solution.py:319
  31.3 0.0 collective-permute-done.1.refs_1_
  31.3 0.3 collective-permute-done.2.refs_2_
  31.6 0.6 copy-done.6
  32.2 2.0 %collective-permute-done.3.refs_3_ = bf16[176,1920]{1,0:T(8,128)(2,1)S(1)} collective-permute-done((bf16[176,1920]{1,0:T(8,128)(2,1)S(1)}, bf16[176,1920]{1,0:T(8,128)(2,1)S(1)}, u32[]{:S(2)}, u32[]{:S(2)}) %collective-permute-start.3) | collective-permute-done | bytes 675872 | tf_op jit(solution)/shard_map/ppermute | solution.py:298
  34.1 0.8 copy-done.7
  35.0 2.2 %collective-permute-start.4 = (bf16[176,1920]{1,0:T(8,128)(2,1)}, bf16[176,1920]{1,0:T(8,128)(2,1)S(1)}, u32[]{:S(2)}, u32[]{:S(2)}) collective-permute-start(bf16[176,1920]{1,0:T(8,128)(2,1)} %collective-permute-done.2.refs_2_), channel_id=1, source_target_pairs={{0,4},{4,0},{1,5},{5,1},{2,6},{6,2},{3,7},{7,3},{8,12},{12,8},{9,1... | collective-permute-start | bytes 2027528 | tf_op jit(solution)/shard_map/ppermute | solution.py:302
  37.2 4.0 %collective-permute-start.5 = (bf16[176,1920]{1,0:T(8,128)(2,1)}, bf16[176,1920]{1,0:T(8,128)(2,1)S(1)}, u32[]{:S(2)}, u32[]{:S(2)}) collective-permute-start(bf16[176,1920]{1,0:T(8,128)(2,1)} %copy-done.6), channel_id=1, source_target_pairs={{0,3},{1,0},{2,1},{3,2},{4,7},{5,4},{6,5},{7,6},{8,11},{9,8},{10,9... | collective-permute-start | bytes 2027528 | tf_op jit(solution)/shard_map/ppermute | solution.py:303
  41.2 1.9 %collective-permute-start.6 = (bf16[176,1920]{1,0:T(8,128)(2,1)}, bf16[176,1920]{1,0:T(8,128)(2,1)}, u32[]{:S(2)}, u32[]{:S(2)}) collective-permute-start(bf16[176,1920]{1,0:T(8,128)(2,1)} %collective-permute-done.2.refs_2_), channel_id=1, source_target_pairs={{0,1},{1,2},{2,3},{3,0},{4,5},{5,6},{6,7},{7,4},{8,9},{9,10},{10,1... | collective-permute-start | bytes 2027528 | tf_op jit(solution)/shard_map/ppermute | solution.py:304
  43.2 0.6 stack.39.place_ref
  43.8 4.7 %collective-permute-done.4.refs_4_ = bf16[176,1920]{1,0:T(8,128)(2,1)S(1)} collective-permute-done((bf16[176,1920]{1,0:T(8,128)(2,1)}, bf16[176,1920]{1,0:T(8,128)(2,1)S(1)}, u32[]{:S(2)}, u32[]{:S(2)}) %collective-permute-start.4) | collective-permute-done | bytes 675872 | tf_op jit(solution)/shard_map/ppermute | solution.py:302
  48.5 3.1 %collective-permute-start.7 = (bf16[80,1920]{1,0:T(8,128)(2,1)S(1)}, bf16[80,1920]{1,0:T(8,128)(2,1)S(1)}, u32[]{:S(2)}, u32[]{:S(2)}) collective-permute-start(bf16[80,1920]{1,0:T(8,128)(2,1)S(1)} %slice.40), channel_id=1, source_target_pairs={{0,1},{1,2},{2,3},{3,0},{4,5},{5,6},{6,7},{7,4},{8,9},{9,10},{10,1... | collective-permute-start | bytes 921608 | tf_op jit(solution)/shard_map/ppermute | solution.py:305
  51.6 0.0 collective-permute-done.5.refs_5_
  51.7 3.9 %collective-permute-start.8 = (bf16[96,1920]{1,0:T(8,128)(2,1)S(1)}, bf16[96,1920]{1,0:T(8,128)(2,1)S(1)}, u32[]{:S(2)}, u32[]{:S(2)}) collective-permute-start(bf16[96,1920]{1,0:T(8,128)(2,1)S(1)} %slice.41), channel_id=1, source_target_pairs={{0,3},{1,0},{2,1},{3,2},{4,7},{5,4},{6,5},{7,6},{8,11},{9,8},{10,9... | collective-permute-start | bytes 1105928 | tf_op jit(solution)/shard_map/ppermute | solution.py:306
  55.6 0.0 collective-permute-done
  55.7 1.3 broadcast_select_fusion.1
  56.9 1.5 pad_maximum_fusion.weight_ref
  58.4 0.0 collective-permute-done.6.refs_6_
  58.4 3.6 %collective-permute-done.7.refs_7_ = bf16[80,1920]{1,0:T(8,128)(2,1)S(1)} collective-permute-done((bf16[80,1920]{1,0:T(8,128)(2,1)S(1)}, bf16[80,1920]{1,0:T(8,128)(2,1)S(1)}, u32[]{:S(2)}, u32[]{:S(2)}) %collective-permute-start.7) | collective-permute-done | bytes 307232 | tf_op jit(solution)/shard_map/ppermute | solution.py:305
  62.0 0.7 copy-done.9
  62.7 0.7 copy-done.8
  63.4 23.8 %group.1 = (f32[112,512]{1,0:T(8,128)}, bf16[128,512]{1,0:T(8,128)(2,1)}, f32[8,128]{1,0:T(8,128)}, bf16[1408,1024]{1,0:T(8,128)(2,1)}, bf16[1408,1408]{1,0:T(8,128)(2,1)}, /*index=5*/bf16[176,1024]{1,0:T(8,128)(2,1)}) custom-call(s32[9]{0:T(128)} %stack.39.place_ref, bf16[832,1024]{1,0:T(8,128)(2,1)} %pad_maximum_fusion.weight_ref, ...), custom_call_target="tpu_custom_call" | custom-call | flops 12000000000 | bytes 20000000 | tf_op jit(solution)/shard_map/group/pallas_call | solution.py:204
  87.3 8.6 %collective-permute-start.9 = (bf16[128,512]{1,0:T(8,128)(2,1)}, bf16[128,512]{1,0:T(8,128)(2,1)S(1)}, u32[]{:S(2)}, u32[]{:S(2)}) collective-permute-start(bf16[128,512]{1,0:T(8,128)(2,1)} %get-tuple-element.17), channel_id=1, source_target_pairs={{0,8},{8,0},{1,9},{9,1},{2,10},{10,2},{3,11},{11,3},{4,12},{12,4},... | collective-permute-start | bytes 393224 | tf_op jit(solution)/shard_map/ppermute | solution.py:334
  95.9 0.2 fusion.6
  96.0 1.0 collective-permute-done.9.came_ref
  97.1 0.7 copy-done.5
  97.7 1.8 %tiles.1 = bf16[48,16,128]{2,1,0:T(8,128)(2,1)} custom-call(f32[112,512]{1,0:T(8,128)} %get-tuple-element.16.mine_ref, bf16[128,512]{1,0:T(8,128)(2,1)} %copy-done.5, f32[8,128]{1,0:T(8,128)} %get-tuple-element.18.loss_ref), custom_call_target="tpu_custom_call" | custom-call | tf_op jit(solution)/shard_map/tiles/pallas_call | solution.py:260
  99.5 21.4 %all-to-all-start.1 = ((bf16[48,16,128]{2,1,0:T(8,128)(2,1)}), bf16[48,16,128]{2,1,0:T(8,128)(2,1)S(1)}, u32[]{:S(2)}, u32[]{:S(2)}) async-start(bf16[48,16,128]{2,1,0:T(8,128)(2,1)} %tiles.1), calls=%async_computation.1 | async-start | bytes 393216 | tf_op jit(solution)/shard_map/all_to_all | solution.py:340
  121.0 2.5 %convolution_convert_fusion = bf16[176,832]{1,0:T(8,128)(2,1)} fusion(bf16[176,1024]{1,0:T(8,128)(2,1)} %get-tuple-element.19, bf16[832,512]{1,0:T(8,128)(2,1)S(1)} %get-tuple-element.23, bf16[832,512]{1,0:T(8,128)(2,1)S(1)} %get-tuple-element.22), kind=kOutput, calls=%fused_computation.2 | convolution fusion | flops 303447040 | bytes 2357248 | tf_op jit(solution)/shard_map/dot_general | solution.py:277
  123.4 14.0 %all-to-all-done.1 = bf16[48,16,128]{2,1,0:T(8,128)(2,1)S(1)} async-done(((bf16[48,16,128]{2,1,0:T(8,128)(2,1)}), bf16[48,16,128]{2,1,0:T(8,128)(2,1)S(1)}, u32[]{:S(2)}, u32[]{:S(2)}) %all-to-all-start.1) | async-done | bytes 196640 | tf_op jit(solution)/shard_map/all_to_all | solution.py:340
  137.4 0.1 convert_reduce_fusion
  137.5 0.1 select_select_fusion
  137.5 0.7 reshape.115
  138.2 5.7 %all-to-all-start.2 = ((bf16[48,16,128]{2,1,0:T(8,128)(2,1)}), bf16[48,16,128]{2,1,0:T(8,128)(2,1)S(1)}, u32[]{:S(2)}, u32[]{:S(2)}) async-start(bf16[48,16,128]{2,1,0:T(8,128)(2,1)} %reshape.115), calls=%async_computation.2 | async-start | bytes 393216 | tf_op jit(solution)/shard_map/all_to_all | solution.py:350
  143.9 3.3 %fusion.2 = (f32[176]{0:T(256)S(1)}, f32[176,1024]{1,0:T(8,128)S(1)}) fusion(bf16[176,1024]{1,0:T(8,128)(2,1)S(1)} %copy-done, f32[176]{0:T(256)S(1)} %add_rsqrt_fusion, bf16[1408,1024]{1,0:T(8,128)(2,1)} %get-tuple-element.21, bf16[1408,1408]{1,0:T(8,128)(2,1)} %get-tuple-element.20, s32[]{:T(128)S(6)} %select_n.102), kind=kOutput, calls=%fused_computation.9 | convolution fusion | flops 508411712 | bytes 4687236 | tf_op jit(solution)/shard_map/dot_general | solution.py:271
  147.2 1.0 fusion.5
  148.2 11.2 %all-to-all-done.2 = bf16[48,16,128]{2,1,0:T(8,128)(2,1)S(1)} async-done(((bf16[48,16,128]{2,1,0:T(8,128)(2,1)}), bf16[48,16,128]{2,1,0:T(8,128)(2,1)S(1)}, u32[]{:S(2)}, u32[]{:S(2)}) %all-to-all-start.2) | async-done | bytes 196640 | tf_op jit(solution)/shard_map/all_to_all | solution.py:350
  159.5 5.3 %all_gather.3 = bf16[112,1024]{1,0:T(8,128)(2,1)S(1)} all-gather(bf16[112,512]{1,0:T(8,128)(2,1)S(1)} %bitcast.32), channel_id=1, replica_groups=mesh['yh'=4,'z'=12,'core'=2,'yl'=2,'x'=4] {'core'}, dimensions={1}, use_global_device_ids=true | all-gather | bytes 344064 | tf_op jit(solution)/shard_map/all_gather | solution.py:354
  164.8 0.8 slice_convert_fusion
  165.6 0.6 convert_reduce_fusion.1
  (26 shorter events, 0.2 us)
Async XLA Ops:
  0.6 7.9 %copy-start.2 = (bf16[176,832]{1,0:T(8,128)(2,1)S(1)}, bf16[176,832]{1,0:T(8,128)(2,1)}, u32[]{:S(2)}) copy-start(bf16[176,832]{1,0:T(8,128)(2,1)} %param.3) | copy-start | bytes 878596
  0.6 7.9 %copy-start = (bf16[176,1024]{1,0:T(8,128)(2,1)S(1)}, bf16[176,1024]{1,0:T(8,128)(2,1)}, u32[]{:S(2)}) copy-start(bf16[176,1024]{1,0:T(8,128)(2,1)} %param.5) | copy-start | bytes 1081348
  2.6 16.1 %all-to-all-start = ((bf16[8,104,512]{2,1,0:T(8,128)(2,1)}), bf16[8,104,512]{2,1,0:T(8,128)(2,1)S(1)}, u32[]{:S(2)}, u32[]{:S(2)}) async-start(bf16[8,104,512]{2,1,0:T(8,128)(2,1)} %broadcast_in_dim.32), calls=%async_computation | async-start | bytes 1703936 | tf_op jit(solution)/shard_map/all_to_all | solution.py:318
  8.8 46.8 %copy-start.1 = (bf16[176,1920]{1,0:T(8,128)(2,1)}, bf16[176,1920]{1,0:T(8,128)(2,1)S(1)}, u32[]{:S(2)}) copy-start(bf16[176,1920]{1,0:T(8,128)(2,1)S(1)} %concatenate.7.refs_0_) | copy-start | bytes 2027524
  8.8 22.4 %collective-permute-start.1 = (bf16[176,1920]{1,0:T(8,128)(2,1)S(1)}, bf16[176,1920]{1,0:T(8,128)(2,1)S(1)}, u32[]{:S(2)}, u32[]{:S(2)}) collective-permute-start(bf16[176,1920]{1,0:T(8,128)(2,1)S(1)} %concatenate.7.refs_0_), channel_id=1, source_target_pairs={{0,4},{4,0},{1,5},{5,1},{2,6},{6,2},{3,7},{7,3},{8,12},{12,8},{9,1... | collective-permute-start | bytes 2027528 | tf_op jit(solution)/shard_map/ppermute | solution.py:296
  12.2 19.3 %collective-permute-start.2 = (bf16[176,1920]{1,0:T(8,128)(2,1)S(1)}, bf16[176,1920]{1,0:T(8,128)(2,1)}, u32[]{:S(2)}, u32[]{:S(2)}) collective-permute-start(bf16[176,1920]{1,0:T(8,128)(2,1)S(1)} %concatenate.7.refs_0_), channel_id=1, source_target_pairs={{0,1},{1,2},{2,3},{3,0},{4,5},{5,6},{6,7},{7,4},{8,9},{9,10},{10,1... | collective-permute-start | bytes 2027528 | tf_op jit(solution)/shard_map/ppermute | solution.py:297
  15.3 18.8 %collective-permute-start.3 = (bf16[176,1920]{1,0:T(8,128)(2,1)S(1)}, bf16[176,1920]{1,0:T(8,128)(2,1)S(1)}, u32[]{:S(2)}, u32[]{:S(2)}) collective-permute-start(bf16[176,1920]{1,0:T(8,128)(2,1)S(1)} %concatenate.7.refs_0_), channel_id=1, source_target_pairs={{0,3},{1,0},{2,1},{3,2},{4,7},{5,4},{6,5},{7,6},{8,11},{9,8},{10,9... | collective-permute-start | bytes 2027528 | tf_op jit(solution)/shard_map/ppermute | solution.py:298
  18.7 36.9 %collective-permute-start = (bf16[832,512]{1,0:T(8,128)(2,1)S(1)}, bf16[832,512]{1,0:T(8,128)(2,1)}, u32[]{:S(2)}, u32[]{:S(2)}) collective-permute-start(bf16[832,512]{1,0:T(8,128)(2,1)S(1)} %bitcast.29), channel_id=1, source_target_pairs={{0,8},{8,0},{1,9},{9,1},{2,10},{10,2},{3,11},{11,3},{4,12},{12,4},... | collective-permute-start | bytes 2555912 | tf_op jit(solution)/shard_map/ppermute | solution.py:319
  31.3 0.9 copy-start.6
  34.1 0.8 copy-start.7
  35.0 13.5 %collective-permute-start.4 = (bf16[176,1920]{1,0:T(8,128)(2,1)}, bf16[176,1920]{1,0:T(8,128)(2,1)S(1)}, u32[]{:S(2)}, u32[]{:S(2)}) collective-permute-start(bf16[176,1920]{1,0:T(8,128)(2,1)} %collective-permute-done.2.refs_2_), channel_id=1, source_target_pairs={{0,4},{4,0},{1,5},{5,1},{2,6},{6,2},{3,7},{7,3},{8,12},{12,8},{9,1... | collective-permute-start | bytes 2027528 | tf_op jit(solution)/shard_map/ppermute | solution.py:302
  37.2 14.4 %collective-permute-start.5 = (bf16[176,1920]{1,0:T(8,128)(2,1)}, bf16[176,1920]{1,0:T(8,128)(2,1)S(1)}, u32[]{:S(2)}, u32[]{:S(2)}) collective-permute-start(bf16[176,1920]{1,0:T(8,128)(2,1)} %copy-done.6), channel_id=1, source_target_pairs={{0,3},{1,0},{2,1},{3,2},{4,7},{5,4},{6,5},{7,6},{8,11},{9,8},{10,9... | collective-permute-start | bytes 2027528 | tf_op jit(solution)/shard_map/ppermute | solution.py:303
  41.2 17.2 %collective-permute-start.6 = (bf16[176,1920]{1,0:T(8,128)(2,1)}, bf16[176,1920]{1,0:T(8,128)(2,1)}, u32[]{:S(2)}, u32[]{:S(2)}) collective-permute-start(bf16[176,1920]{1,0:T(8,128)(2,1)} %collective-permute-done.2.refs_2_), channel_id=1, source_target_pairs={{0,1},{1,2},{2,3},{3,0},{4,5},{5,6},{6,7},{7,4},{8,9},{9,10},{10,1... | collective-permute-start | bytes 2027528 | tf_op jit(solution)/shard_map/ppermute | solution.py:304
  48.5 7.1 %copy-start.4 = (bf16[176,1920]{1,0:T(8,128)(2,1)}, bf16[176,1920]{1,0:T(8,128)(2,1)S(1)}, u32[]{:S(2)}) copy-start(bf16[176,1920]{1,0:T(8,128)(2,1)S(1)} %collective-permute-done.4.refs_4_) | copy-start | bytes 2027524
  48.5 13.4 %collective-permute-start.7 = (bf16[80,1920]{1,0:T(8,128)(2,1)S(1)}, bf16[80,1920]{1,0:T(8,128)(2,1)S(1)}, u32[]{:S(2)}, u32[]{:S(2)}) collective-permute-start(bf16[80,1920]{1,0:T(8,128)(2,1)S(1)} %slice.40), channel_id=1, source_target_pairs={{0,1},{1,2},{2,3},{3,0},{4,5},{5,6},{6,7},{7,4},{8,9},{9,10},{10,1... | collective-permute-start | bytes 921608 | tf_op jit(solution)/shard_map/ppermute | solution.py:305
  51.6 4.0 %copy-start.3 = (bf16[176,1920]{1,0:T(8,128)(2,1)}, bf16[176,1920]{1,0:T(8,128)(2,1)S(1)}, u32[]{:S(2)}) copy-start(bf16[176,1920]{1,0:T(8,128)(2,1)S(1)} %collective-permute-done.5.refs_5_) | copy-start | bytes 2027524
  51.7 10.3 %collective-permute-start.8 = (bf16[96,1920]{1,0:T(8,128)(2,1)S(1)}, bf16[96,1920]{1,0:T(8,128)(2,1)S(1)}, u32[]{:S(2)}, u32[]{:S(2)}) collective-permute-start(bf16[96,1920]{1,0:T(8,128)(2,1)S(1)} %slice.41), channel_id=1, source_target_pairs={{0,3},{1,0},{2,1},{3,2},{4,7},{5,4},{6,5},{7,6},{8,11},{9,8},{10,9... | collective-permute-start | bytes 1105928 | tf_op jit(solution)/shard_map/ppermute | solution.py:306
  62.0 0.7 copy-start.9
  62.7 0.7 copy-start.8
  87.3 9.8 %collective-permute-start.9 = (bf16[128,512]{1,0:T(8,128)(2,1)}, bf16[128,512]{1,0:T(8,128)(2,1)S(1)}, u32[]{:S(2)}, u32[]{:S(2)}) collective-permute-start(bf16[128,512]{1,0:T(8,128)(2,1)} %get-tuple-element.17), channel_id=1, source_target_pairs={{0,8},{8,0},{1,9},{9,1},{2,10},{10,2},{3,11},{11,3},{4,12},{12,4},... | collective-permute-start | bytes 393224 | tf_op jit(solution)/shard_map/ppermute | solution.py:334
  97.1 0.7 copy-start.5
  99.5 37.9 %all-to-all-start.1 = ((bf16[48,16,128]{2,1,0:T(8,128)(2,1)}), bf16[48,16,128]{2,1,0:T(8,128)(2,1)S(1)}, u32[]{:S(2)}, u32[]{:S(2)}) async-start(bf16[48,16,128]{2,1,0:T(8,128)(2,1)} %tiles.1), calls=%async_computation.1 | async-start | bytes 393216 | tf_op jit(solution)/shard_map/all_to_all | solution.py:340
  138.2 21.2 %all-to-all-start.2 = ((bf16[48,16,128]{2,1,0:T(8,128)(2,1)}), bf16[48,16,128]{2,1,0:T(8,128)(2,1)S(1)}, u32[]{:S(2)}, u32[]{:S(2)}) async-start(bf16[48,16,128]{2,1,0:T(8,128)(2,1)} %reshape.115), calls=%async_computation.2 | async-start | bytes 393216 | tf_op jit(solution)/shard_map/all_to_all | solution.py:350
